TPU v7x, 32 devices: a whole 2x2x4 slice. The times are simulated.
32 devices in a mesh: page: 8 (over y, x, core), band: 4 (over z).
Axes of the slice: x: 2, y: 2, z: 4, core: 2. Of those that a mesh axis runs over, the one named last changes fastest.
Arguments:
- hidden_in: bfloat16 [10240, 768], P(('page', 'band')), may hold values from -6 to 6
- lengths: int32 [8, 40], P('page'), may hold values from 1 to 512, 1280 in all within a row
- permutation: int32 [8, 1280], P('page', 'band'), may hold values from 0 to 1279, as said below
- query_weight: float32 [768, 768], P(('page', 'band')), may hold values from -0.21875 to 0.21875
- query_bias: float32 [768], P(('page', 'band')), may hold values from -3 to 3
- key_weight: float32 [768, 768], P(('page', 'band')), may hold values from -0.21875 to 0.21875
- value_weight: float32 [768, 768], P(('page', 'band')), may hold values from -0.21875 to 0.21875
- value_bias: float32 [768], P(('page', 'band')), may hold values from -3 to 3
- mix_weight: float32 [768, 768], P(('page', 'band')), may hold values from -0.875 to 0.875
- mix_bias: float32 [768], P(('page', 'band')), may hold values from -3 to 3
- first_gain: float32 [768], P(('page', 'band')), may hold values from 0.4 to 1.6
- first_shift: float32 [768], P(('page', 'band')), may hold values from -3 to 3
- expand_weight: float32 [768, 3072], P(('page', 'band')), may hold values from -0.21875 to 0.21875
- expand_bias: float32 [3072], P(('page', 'band')), may hold values from -3 to 3
- contract_weight: float32 [3072, 768], P(('page', 'band')), may hold values from -0.21875 to 0.21875
- contract_bias: float32 [768], P(('page', 'band')), may hold values from -3 to 3
- second_gain: float32 [768], P(('page', 'band')), may hold values from 0.4 to 1.6
- second_shift: float32 [768], P(('page', 'band')), may hold values from -3 to 3
- cotangent: bfloat16 [10240, 768], P(('page', 'band')), may hold values from -6 to 6
Outputs:
- layer_output: bfloat16 [10240, 768], P(('page', 'band'))
- input_gradient: bfloat16 [10240, 768], P(('page', 'band'))
- query_weight_gradient: float32 [768, 768], P(('page', 'band'))
- query_bias_gradient: float32 [768], P(('page', 'band'))
- key_weight_gradient: float32 [768, 768], P(('page', 'band'))
- value_weight_gradient: float32 [768, 768], P(('page', 'band'))
- value_bias_gradient: float32 [768], P(('page', 'band'))
- mix_weight_gradient: float32 [768, 768], P(('page', 'band'))
- mix_bias_gradient: float32 [768], P(('page', 'band'))
- first_gain_gradient: float32 [768], P(('page', 'band'))
- first_shift_gradient: float32 [768], P(('page', 'band'))
- expand_weight_gradient: float32 [768, 3072], P(('page', 'band'))
- expand_bias_gradient: float32 [3072], P(('page', 'band'))
- contract_weight_gradient: float32 [3072, 768], P(('page', 'band'))
- contract_bias_gradient: float32 [768], P(('page', 'band'))
- second_gain_gradient: float32 [768], P(('page', 'band'))
- second_shift_gradient: float32 [768], P(('page', 'band'))
Inputs may be any that keep to these rules, and one draw needn't show every extreme that they name: Each row lists the 40 document lengths of one page group; they sum to 1280, and the longest is exactly 512. Each row is a permutation of 0 .. 1279; the positions k * 1280 // 320 to (k + 1) * 1280 // 320 - 1 lie in slots of different bands, one on each.
All inputs are finite; a program needn't handle non-finite values.
Results may differ from a plain program's by a relative error of at most 0.017.
Values may be sent and summed in bfloat16 or wider, within the bound.
No kernel may reach another device: no remote copies, remote signals or barrier semaphores. Data moves between devices by JAX's collectives and lax.ppermute only.
A program may use at most 192 MiB of HBM per device.

v0:
```python
import jax
import jax.numpy as jnp
from jax import lax
from jax.sharding import PartitionSpec as P

HEAD_DIM = 64


EPSILON = 1e-12


def times_transposed(left, right):
    return lax.dot_general(
        left, right, (((1,), (1,)), ((), ())), preferred_element_type=jnp.float32
    )


def outer_sum(left, right):
    return lax.dot_general(
        left, right, (((0,), (0,)), ((), ())), preferred_element_type=jnp.float32
    )


def exact_gelu(values):
    return jax.nn.gelu(values, approximate=False)


def layer_norm(inputs, scale_gain, shift_bias):
    centred = inputs - jnp.mean(inputs, axis=-1, keepdims=True)
    variance = jnp.mean(centred * centred, axis=-1, keepdims=True)
    inverse = lax.rsqrt(variance + EPSILON)
    normed = centred * inverse
    return (normed * scale_gain + shift_bias, normed, inverse)


def norm_back(grad_out, normed, inverse, scale_gain):
    grad_normed = grad_out * scale_gain
    inner = (
        grad_normed
        - jnp.mean(grad_normed, axis=-1, keepdims=True)
        - normed * jnp.mean(grad_normed * normed, axis=-1, keepdims=True)
    )
    return (inner * inverse, jnp.sum(grad_out * normed, axis=0), jnp.sum(grad_out, axis=0))


def head_slice(matrix, pair_index, pair_width):
    block = lax.dynamic_slice_in_dim(matrix, pair_index * pair_width, pair_width, 1)
    return block.reshape(matrix.shape[0], 2, pair_width // 2)


def to_columns(pieces):
    return jnp.transpose(pieces, (1, 0, 2)).reshape(
        pieces.shape[1], pieces.shape[0] * pieces.shape[2]
    )


def per_device(
    hidden_in,
    lengths,
    permutation,
    query_weight,
    query_bias,
    key_weight,
    value_weight,
    value_bias,
    mix_weight,
    mix_bias,
    first_gain,
    first_shift,
    expand_weight,
    expand_bias,
    contract_weight,
    contract_bias,
    second_gain,
    second_shift,
    cotangent,
):
    low_masters = tuple(
        (
            item.astype(jnp.bfloat16)
            for item in (
                query_weight,
                query_bias,
                key_weight,
                value_weight,
                value_bias,
                mix_weight,
                mix_bias,
                first_gain,
                first_shift,
                expand_weight,
                expand_bias,
                contract_weight,
                contract_bias,
                second_gain,
                second_shift,
            )
        )
    )
    gathered = (
        lax.all_gather(low_masters[0], ("page", "band"), axis=0, tiled=True),
        lax.all_gather(low_masters[1], ("page", "band"), axis=0, tiled=True),
        lax.all_gather(low_masters[2], ("page", "band"), axis=0, tiled=True),
        lax.all_gather(low_masters[3], ("page", "band"), axis=0, tiled=True),
        lax.all_gather(low_masters[4], ("page", "band"), axis=0, tiled=True),
        lax.all_gather(low_masters[5], ("page", "band"), axis=0, tiled=True),
        lax.all_gather(low_masters[6], ("page", "band"), axis=0, tiled=True),
        lax.all_gather(low_masters[7], ("page", "band"), axis=0, tiled=True),
        lax.all_gather(low_masters[8], ("page", "band"), axis=0, tiled=True),
        lax.all_gather(low_masters[9], ("page", "band"), axis=0, tiled=True),
        lax.all_gather(low_masters[10], ("page", "band"), axis=0, tiled=True),
        lax.all_gather(low_masters[11], ("page", "band"), axis=0, tiled=True),
        lax.all_gather(low_masters[12], ("page", "band"), axis=0, tiled=True),
        lax.all_gather(low_masters[13], ("page", "band"), axis=0, tiled=True),
        lax.all_gather(low_masters[14], ("page", "band"), axis=0, tiled=True),
    )
    (
        w_query,
        b_query,
        w_key,
        w_value,
        b_value,
        w_mix,
        b_mix,
        gain_one,
        shift_one,
        w_expand,
        b_expand,
        w_contract,
        b_contract,
        gain_two,
        shift_two,
    ) = gathered
    token_count = hidden_in.shape[0]
    width = hidden_in.shape[1]
    pair_width = 2 * HEAD_DIM
    pair_count = width // pair_width
    scale_factor = HEAD_DIM ** (-0.5)
    ends = jnp.cumsum(lengths[0])
    local_docs = jnp.sum((permutation[0][:, None] >= ends[None, :]).astype(jnp.int32), axis=1)
    doc_marks = local_docs.astype(jnp.bfloat16)
    query_low = (
        jnp.dot(hidden_in, w_query, preferred_element_type=jnp.float32)
        + b_query.astype(jnp.float32)
    ).astype(jnp.bfloat16)
    key_low = jnp.dot(hidden_in, w_key, preferred_element_type=jnp.float32).astype(jnp.bfloat16)
    value_low = (
        jnp.dot(hidden_in, w_value, preferred_element_type=jnp.float32)
        + b_value.astype(jnp.float32)
    ).astype(jnp.bfloat16)
    keys_all, values_all, marks_all = (
        lax.all_gather(key_low, "band", axis=0, tiled=True),
        lax.all_gather(value_low, "band", axis=0, tiled=True),
        lax.all_gather(doc_marks, "band", axis=0, tiled=True),
    )
    same_doc = (doc_marks[:, None] == marks_all[None, :])[None]

    def pair_scores(pair_index):
        query_part = head_slice(query_low, pair_index, pair_width)
        key_part = head_slice(keys_all, pair_index, pair_width)
        value_part = head_slice(values_all, pair_index, pair_width)
        raw_scores = jnp.einsum(
            "qhd,khd->hqk", query_part, key_part, preferred_element_type=jnp.float32
        )
        return (
            query_part,
            key_part,
            value_part,
            jnp.where(same_doc, raw_scores * scale_factor, -1e30),
        )

    def forward_pair(pair_index):
        query_part, key_part, value_part, scores = pair_scores(pair_index)
        row_peak = jnp.max(scores, axis=-1, keepdims=True)
        unscaled = jnp.exp(scores - row_peak)
        row_total = jnp.sum(unscaled, axis=-1, keepdims=True)
        weights_low = (unscaled / row_total).astype(jnp.bfloat16)
        pair_out = jnp.einsum(
            "hqk,khd->qhd", weights_low, value_part, preferred_element_type=jnp.float32
        )
        return (
            pair_out.reshape(token_count, pair_width),
            row_peak[..., 0] + jnp.log(row_total[..., 0]),
        )

    pieces, log_totals = lax.map(forward_pair, jnp.arange(pair_count))
    attended_low = to_columns(pieces).astype(jnp.bfloat16)
    mix_out = jnp.dot(attended_low, w_mix, preferred_element_type=jnp.float32) + b_mix.astype(
        jnp.float32
    )
    gain_first = gain_one.astype(jnp.float32)
    first, first_normed, first_inverse = layer_norm(
        hidden_in.astype(jnp.float32) + mix_out, gain_first, shift_one.astype(jnp.float32)
    )
    first_low = first.astype(jnp.bfloat16)
    expanded = jnp.dot(first_low, w_expand, preferred_element_type=jnp.float32) + b_expand.astype(
        jnp.float32
    )
    activated, gelu_back = jax.vjp(exact_gelu, expanded)
    activated_low = activated.astype(jnp.bfloat16)
    contracted = jnp.dot(
        activated_low, w_contract, preferred_element_type=jnp.float32
    ) + b_contract.astype(jnp.float32)
    gain_second = gain_two.astype(jnp.float32)
    result, second_normed, second_inverse = layer_norm(
        first + contracted, gain_second, shift_two.astype(jnp.float32)
    )
    grad_second, grad_gain_two, grad_shift_two = norm_back(
        cotangent.astype(jnp.float32), second_normed, second_inverse, gain_second
    )
    grad_contract_low = grad_second.astype(jnp.bfloat16)
    grad_w_contract = outer_sum(activated_low, grad_contract_low)
    grad_b_contract = jnp.sum(grad_contract_low.astype(jnp.float32), axis=0)
    grad_activated = times_transposed(grad_contract_low, w_contract)
    grad_expanded_low = gelu_back(grad_activated)[0].astype(jnp.bfloat16)
    grad_w_expand = outer_sum(first_low, grad_expanded_low)
    grad_b_expand = jnp.sum(grad_expanded_low.astype(jnp.float32), axis=0)
    grad_first = grad_second + times_transposed(grad_expanded_low, w_expand)
    grad_first_sum, grad_gain_one, grad_shift_one = norm_back(
        grad_first, first_normed, first_inverse, gain_first
    )
    grad_mixed_low = grad_first_sum.astype(jnp.bfloat16)
    grad_w_mix = outer_sum(attended_low, grad_mixed_low)
    grad_b_mix = jnp.sum(grad_mixed_low.astype(jnp.float32), axis=0)
    grad_attended_low = times_transposed(grad_mixed_low, w_mix).astype(jnp.bfloat16)

    def backward_pair(pair_index):
        query_part, key_part, value_part, scores = pair_scores(pair_index)
        attention_weights = jnp.exp(scores - log_totals[pair_index][..., None])
        weights_low = attention_weights.astype(jnp.bfloat16)
        grad_part = head_slice(grad_attended_low, pair_index, pair_width)
        grad_weights = jnp.einsum(
            "qhd,khd->hqk", grad_part, value_part, preferred_element_type=jnp.float32
        )
        grad_scores = attention_weights * (
            grad_weights - jnp.sum(attention_weights * grad_weights, axis=-1, keepdims=True)
        )
        grad_raw_low = (grad_scores * scale_factor).astype(jnp.bfloat16)
        grad_query_part = jnp.einsum(
            "hqk,khd->qhd", grad_raw_low, key_part, preferred_element_type=jnp.float32
        )
        grad_key_part = jnp.einsum(
            "hqk,qhd->khd", grad_raw_low, query_part, preferred_element_type=jnp.float32
        )
        grad_value_part = jnp.einsum(
            "hqk,qhd->khd", weights_low, grad_part, preferred_element_type=jnp.float32
        )
        key_count = grad_key_part.shape[0]
        own_keys, own_values = (
            lax.psum_scatter(
                grad_key_part.reshape(key_count, pair_width).astype(jnp.bfloat16),
                "band",
                scatter_dimension=0,
                tiled=True,
            ).astype(jnp.float32),
            lax.psum_scatter(
                grad_value_part.reshape(key_count, pair_width).astype(jnp.bfloat16),
                "band",
                scatter_dimension=0,
                tiled=True,
            ).astype(jnp.float32),
        )
        return (grad_query_part.reshape(token_count, pair_width), own_keys, own_values)

    query_pieces, key_pieces, value_pieces = lax.map(backward_pair, jnp.arange(pair_count))
    grad_query_low = to_columns(query_pieces).astype(jnp.bfloat16)
    grad_key_low = to_columns(key_pieces).astype(jnp.bfloat16)
    grad_value_low = to_columns(value_pieces).astype(jnp.bfloat16)
    grad_w_query = outer_sum(hidden_in, grad_query_low)
    grad_b_query = jnp.sum(grad_query_low.astype(jnp.float32), axis=0)
    grad_w_key = outer_sum(hidden_in, grad_key_low)
    grad_w_value = outer_sum(hidden_in, grad_value_low)
    grad_b_value = jnp.sum(grad_value_low.astype(jnp.float32), axis=0)
    grad_input = (
        grad_first_sum
        + times_transposed(grad_query_low, w_query)
        + times_transposed(grad_key_low, w_key)
        + times_transposed(grad_value_low, w_value)
    )
    summed = (
        lax.psum_scatter(grad_w_query, ("page", "band"), scatter_dimension=0, tiled=True),
        lax.psum_scatter(grad_b_query, ("page", "band"), scatter_dimension=0, tiled=True),
        lax.psum_scatter(grad_w_key, ("page", "band"), scatter_dimension=0, tiled=True),
        lax.psum_scatter(grad_w_value, ("page", "band"), scatter_dimension=0, tiled=True),
        lax.psum_scatter(grad_b_value, ("page", "band"), scatter_dimension=0, tiled=True),
        lax.psum_scatter(grad_w_mix, ("page", "band"), scatter_dimension=0, tiled=True),
        lax.psum_scatter(grad_b_mix, ("page", "band"), scatter_dimension=0, tiled=True),
        lax.psum_scatter(grad_gain_one, ("page", "band"), scatter_dimension=0, tiled=True),
        lax.psum_scatter(grad_shift_one, ("page", "band"), scatter_dimension=0, tiled=True),
        lax.psum_scatter(grad_w_expand, ("page", "band"), scatter_dimension=0, tiled=True),
        lax.psum_scatter(grad_b_expand, ("page", "band"), scatter_dimension=0, tiled=True),
        lax.psum_scatter(grad_w_contract, ("page", "band"), scatter_dimension=0, tiled=True),
        lax.psum_scatter(grad_b_contract, ("page", "band"), scatter_dimension=0, tiled=True),
        lax.psum_scatter(grad_gain_two, ("page", "band"), scatter_dimension=0, tiled=True),
        lax.psum_scatter(grad_shift_two, ("page", "band"), scatter_dimension=0, tiled=True),
    )
    return (
        result.astype(jnp.bfloat16),
        grad_input.astype(jnp.bfloat16),
        summed[0],
        summed[1],
        summed[2],
        summed[3],
        summed[4],
        summed[5],
        summed[6],
        summed[7],
        summed[8],
        summed[9],
        summed[10],
        summed[11],
        summed[12],
        summed[13],
        summed[14],
    )


def solution(mesh):
    in_specs = (
        P(("page", "band"), None),
        P("page", None),
        P("page", "band"),
        P(("page", "band"), None),
        P(("page", "band")),
        P(("page", "band"), None),
        P(("page", "band"), None),
        P(("page", "band")),
        P(("page", "band"), None),
        P(("page", "band")),
        P(("page", "band")),
        P(("page", "band")),
        P(("page", "band"), None),
        P(("page", "band")),
        P(("page", "band"), None),
        P(("page", "band")),
        P(("page", "band")),
        P(("page", "band")),
        P(("page", "band"), None),
    )
    out_specs = (
        P(("page", "band"), None),
        P(("page", "band"), None),
        P(("page", "band"), None),
        P(("page", "band")),
        P(("page", "band"), None),
        P(("page", "band"), None),
        P(("page", "band")),
        P(("page", "band"), None),
        P(("page", "band")),
        P(("page", "band")),
        P(("page", "band")),
        P(("page", "band"), None),
        P(("page", "band")),
        P(("page", "band"), None),
        P(("page", "band")),
        P(("page", "band")),
        P(("page", "band")),
    )
    return jax.shard_map(
        per_device, mesh=mesh, in_specs=in_specs, out_specs=out_specs, check_vma=False
    )
```

profile of v0, /device:TPU:0, one launch (start us, length us, event | category | flops | bytes accessed | tf_op | source)
XLA Modules:
  0.0 1541.3 jit_solution(14951937770082840441)
XLA Ops:
  19.9 42.7 %all-reduce.20 = (bf16[3072]{0:T(1024)(128)(2,1)S(1)}, bf16[768]{0:T(1024)(128)(2,1)S(1)}, bf16[768]{0:T(1024)(128)(2,1)S(1)}, bf16[768]{0:T(1024)(128)(2,1)S(1)...) all-reduce(bf16[3072]{0:T(1024)(128)(2,1)S(1)} %dynamic-update-slic, ...), channel_id=1, replica_groups=mesh['page'=8,'band'=4] {'page','band'}, use_global_device_ids=true, to_apply=%add.6 | all-reduce | flops 9216 | bytes 36864
  71.2 53.8 %all-gather.15.cloned.1.call-done = bf16[768,768]{1,0:T(8,128)(2,1)} async-done(((bf16[24,768]{1,0:T(8,128)(2,1)}), bf16[768,768]{1,0:T(8,128)(2,1)}) %all-gather.15.cloned.1.call-update) | async-done | bytes 1179664 | tf_op jit(solution)/shard_map/all_gather | solution.py:103
  132.0 10.8 all-reduce.1
  142.9 38.6 %all-gather.13.cloned.1.call-done = bf16[768,768]{1,0:T(8,128)(2,1)} async-done(((bf16[24,768]{1,0:T(8,128)(2,1)}), bf16[768,768]{1,0:T(8,128)(2,1)}) %all-gather.13.cloned.1.call-update) | async-done | bytes 1179664 | tf_op jit(solution)/shard_map/all_gather | solution.py:101
  184.4 41.6 %all-gather.11.cloned.1.call-done = bf16[1280,768]{1,0:T(8,128)(2,1)} async-done(((bf16[320,768]{1,0:T(8,128)(2,1)}), bf16[1280,768]{1,0:T(8,128)(2,1)}) %all-gather.11.cloned.1.call-update) | async-done | bytes 1966096 | tf_op jit(solution)/shard_map/all_gather | solution.py:153
  230.0 40.4 %all-gather.17.cloned.1.call-done = bf16[1280,768]{1,0:T(8,128)(2,1)} async-done(((bf16[320,768]{1,0:T(8,128)(2,1)}), bf16[1280,768]{1,0:T(8,128)(2,1)}) %all-gather.17.cloned.1.call-update) | async-done | bytes 1966096 | tf_op jit(solution)/shard_map/all_gather | solution.py:152
  274.5 36.1 %while.28 = (s32[]{:T(128)}, bf16[6,320,128]{1,2,0:T(8,128)(2,1)S(1)}, f32[6,2,320]{2,1,0:T(2,128)S(1)}, s32[6]{0:T(128)S(1)}, bf16[1280,768]{0,1:T(8,128)(2,1)}...) while((s32[]{:T(128)}, ...), condition=%wide.region_5.6_spmd.clone, body=%wide.region_2.5_spmd.clone.sunk | while | flops 216677760 | bytes 13165383 | solution.py:186
  310.6 16.0 %all-gather.19.cloned.1.call-done = bf16[768,768]{1,0:T(8,128)(2,1)} async-done(((bf16[24,768]{1,0:T(8,128)(2,1)}), bf16[768,768]{1,0:T(8,128)(2,1)}) %all-gather.19.cloned.1.call-update) | async-done | bytes 1179664 | tf_op jit(solution)/shard_map/all_gather | solution.py:106
  328.9 63.7 %all-gather.21.cloned.1.call-done = bf16[768,3072]{1,0:T(8,128)(2,1)} async-done(((bf16[24,3072]{1,0:T(8,128)(2,1)}), bf16[768,3072]{1,0:T(8,128)(2,1)}) %all-gather.21.cloned.1.call-update) | async-done | bytes 4718608 | tf_op jit(solution)/shard_map/all_gather | solution.py:110
  392.6 13.5 multiply_convert_fusion
  406.0 52.4 %all-gather.23.cloned.1.call-done = bf16[3072,768]{1,0:T(8,128)(2,1)} async-done(((bf16[96,768]{1,0:T(8,128)(2,1)}), bf16[3072,768]{1,0:T(8,128)(2,1)}) %all-gather.23.cloned.1.call-update) | async-done | bytes 4718608 | tf_op jit(solution)/shard_map/all_gather | solution.py:112
  481.0 352.8 %while.29 = (s32[]{:T(128)}, bf16[6,320,128]{1,2,0:T(8,128)(2,1)}, bf16[6,320,128]{1,2,0:T(8,128)(2,1)}, bf16[6,320,128]{1,2,0:T(8,128)(2,1)}, s32[6]{0:T(128)S(...) while((s32[]{:T(128)}, bf16[6,320,128]{1,2,0:T(8,128)(2,1)}, ...), condition=%wide.region_18.19_spmd.clone, body=%wide.region_14.18_spmd.clone.sunk | while | flops 536579840 | bytes 33762312 | solution.py:265
  508.7 9.5 reduce-scatter.35.cloned.1.call-done
  519.8 18.7 %reduce-scatter.37.cloned.1.call-done = bf16[320,128]{1,0:T(8,128)(2,1)} async-done(((bf16[1280,128]{1,0:T(8,128)(2,1)}), bf16[320,128]{1,0:T(8,128)(2,1)}) %reduce-scatter.37.cloned.1.call-update) | async-done | bytes 81936 | tf_op jit(solution)/shard_map/while
  567.9 8.9 reduce-scatter.35.cloned.1.call-done
  578.5 18.8 %reduce-scatter.37.cloned.1.call-done = bf16[320,128]{1,0:T(8,128)(2,1)} async-done(((bf16[1280,128]{1,0:T(8,128)(2,1)}), bf16[320,128]{1,0:T(8,128)(2,1)}) %reduce-scatter.37.cloned.1.call-update) | async-done | bytes 81936 | tf_op jit(solution)/shard_map/while
  626.7 8.9 reduce-scatter.35.cloned.1.call-done
  637.2 18.8 %reduce-scatter.37.cloned.1.call-done = bf16[320,128]{1,0:T(8,128)(2,1)} async-done(((bf16[1280,128]{1,0:T(8,128)(2,1)}), bf16[320,128]{1,0:T(8,128)(2,1)}) %reduce-scatter.37.cloned.1.call-update) | async-done | bytes 81936 | tf_op jit(solution)/shard_map/while
  685.4 8.9 reduce-scatter.35.cloned.1.call-done
  696.0 18.8 %reduce-scatter.37.cloned.1.call-done = bf16[320,128]{1,0:T(8,128)(2,1)} async-done(((bf16[1280,128]{1,0:T(8,128)(2,1)}), bf16[320,128]{1,0:T(8,128)(2,1)}) %reduce-scatter.37.cloned.1.call-update) | async-done | bytes 81936 | tf_op jit(solution)/shard_map/while
  744.2 8.9 reduce-scatter.35.cloned.1.call-done
  754.7 18.8 %reduce-scatter.37.cloned.1.call-done = bf16[320,128]{1,0:T(8,128)(2,1)} async-done(((bf16[1280,128]{1,0:T(8,128)(2,1)}), bf16[320,128]{1,0:T(8,128)(2,1)}) %reduce-scatter.37.cloned.1.call-update) | async-done | bytes 81936 | tf_op jit(solution)/shard_map/while
  802.8 8.9 reduce-scatter.35.cloned.1.call-done
  813.3 18.8 %reduce-scatter.37.cloned.1.call-done = bf16[320,128]{1,0:T(8,128)(2,1)} async-done(((bf16[1280,128]{1,0:T(8,128)(2,1)}), bf16[320,128]{1,0:T(8,128)(2,1)}) %reduce-scatter.37.cloned.1.call-update) | async-done | bytes 81936 | tf_op jit(solution)/shard_map/while
  845.7 8.3 fusion.56
  864.6 39.8 %all-reduce.19 = (f32[768]{0:T(1024)S(1)}, f32[768]{0:T(1024)S(1)}, f32[768]{0:T(1024)S(1)}, f32[768]{0:T(1024)S(1)}, f32[768]{0:T(1024)S(1)}, /*index=5*/f32[30...) all-reduce(f32[768]{0:T(1024)S(1)} %bitcast.182, ...), channel_id=5, replica_groups=mesh['page'=8,'band'=4] {'page','band'}, use_global_device_ids=true, to_apply=%region_21.22.clone | all-reduce | flops 9216 | bytes 73728
  913.9 23.9 %reduce-scatter.23.cloned.1.call-done = f32[24,768]{1,0:T(8,128)} async-done(((f32[768,768]{1,0:T(8,128)}), f32[24,768]{1,0:T(8,128)}) %reduce-scatter.23.cloned.1.call-update) | async-done | bytes 73744 | tf_op jit(solution)/shard_map/reduce_scatter | solution.py:286
  937.9 104.8 %reduce-scatter.29.cloned.1.call-done = f32[24,768]{1,0:T(8,128)} async-done(((f32[768,768]{1,0:T(8,128)}), f32[24,768]{1,0:T(8,128)}) %reduce-scatter.29.cloned.1.call-update) | async-done | bytes 73744
  1042.6 103.9 %reduce-scatter.31.cloned.1.call-done = f32[24,768]{1,0:T(8,128)} async-done(((f32[768,768]{1,0:T(8,128)}), f32[24,768]{1,0:T(8,128)}) %reduce-scatter.31.cloned.1.call-update) | async-done | bytes 73744
  1146.6 104.6 %reduce-scatter.33.cloned.1.call-done = f32[24,768]{1,0:T(8,128)} async-done(((f32[768,768]{1,0:T(8,128)}), f32[24,768]{1,0:T(8,128)}) %reduce-scatter.33.cloned.1.call-update) | async-done | bytes 73744
  1251.2 141.2 %reduce-scatter.25.cloned.1.call-done = f32[24,3072]{1,0:T(8,128)} async-done(((f32[768,3072]{1,0:T(8,128)}), f32[24,3072]{1,0:T(8,128)}) %reduce-scatter.25.cloned.1.call-update) | async-done | bytes 294928 | tf_op jit(solution)/shard_map/reduce_scatter | solution.py:290
  1392.4 141.9 %reduce-scatter.27.cloned.1.call-done = f32[96,768]{1,0:T(8,128)} async-done(((f32[3072,768]{1,0:T(8,128)}), f32[96,768]{1,0:T(8,128)}) %reduce-scatter.27.cloned.1.call-update) | async-done | bytes 294928 | tf_op jit(solution)/shard_map/reduce_scatter | solution.py:292
  (404 shorter events, 296.7 us)
Async XLA Ops:
  7.2 120.7 %copy-start.17 = (f32[24,768]{1,0:T(8,128)S(1)}, f32[24,768]{1,0:T(8,128)}, u32[]{:S(2)}) copy-start(f32[24,768]{1,0:T(8,128)} %param.31) | copy-start | bytes 221188
  7.2 121.4 %copy-start.15 = (f32[24,3072]{1,0:T(8,128)S(1)}, f32[24,3072]{1,0:T(8,128)}, u32[]{:S(2)}) copy-start(f32[24,3072]{1,0:T(8,128)} %param.35) | copy-start | bytes 884740
  7.2 122.1 %copy-start.16 = (f32[96,768]{1,0:T(8,128)S(1)}, f32[96,768]{1,0:T(8,128)}, u32[]{:S(2)}) copy-start(f32[96,768]{1,0:T(8,128)} %param.37) | copy-start | bytes 884740
  7.2 61.2 %all-gather.9.cloned.1.call-start = ((), (), s32[]{:S(2)}) async-start(), calls=%async_computation.8 | async-start | bytes 1216512 | tf_op jit(solution)/shard_map/all_gather | solution.py:104
  8.9 121.2 %copy-start.26 = (s32[1,40]{1,0:T(1,128)S(1)}, s32[1,40]{1,0:T(1,128)}, u32[]{:S(2)}) copy-start(s32[1,40]{1,0:T(1,128)} %param.24) | copy-start | bytes 484
  8.9 116.2 %all-gather.15.cloned.1.call-start = ((), (), s32[]{:S(2)}) async-start(), calls=%async_computation.11 | async-start | bytes 1216512 | tf_op jit(solution)/shard_map/all_gather | solution.py:103
  10.5 171.0 %copy-start.7 = (bf16[320,768]{1,0:T(8,128)(2,1)S(1)}, bf16[320,768]{1,0:T(8,128)(2,1)}, u32[]{:S(2)}) copy-start(bf16[320,768]{1,0:T(8,128)(2,1)} %param.23) | copy-start | bytes 1474564
  10.5 171.0 %all-gather.13.cloned.1.call-start = ((), (), s32[]{:S(2)}) async-start(), calls=%async_computation.10 | async-start | bytes 1216512 | tf_op jit(solution)/shard_map/all_gather | solution.py:101
  12.1 213.9 %all-gather.11.cloned.1.call-start = ((), (), s32[]{:S(2)}) async-start(), calls=%async_computation.9 | async-start | bytes 2457600 | tf_op jit(solution)/shard_map/all_gather | solution.py:153
  71.2 199.3 %all-gather.17.cloned.1.call-start = ((), (), s32[]{:S(2)}) async-start(), calls=%async_computation.12 | async-start | bytes 2457600 | tf_op jit(solution)/shard_map/all_gather | solution.py:152
  127.8 198.8 %all-gather.19.cloned.1.call-start = ((), (), s32[]{:S(2)}) async-start(), calls=%async_computation.13 | async-start | bytes 1216512 | tf_op jit(solution)/shard_map/all_gather | solution.py:106
  128.5 264.0 %all-gather.21.cloned.1.call-start = ((), (), s32[]{:S(2)}) async-start(), calls=%async_computation.14 | async-start | bytes 4866048 | tf_op jit(solution)/shard_map/all_gather | solution.py:110
  129.3 329.1 %all-gather.23.cloned.1.call-start = ((), (), s32[]{:S(2)}) async-start(), calls=%async_computation.15 | async-start | bytes 4866048 | tf_op jit(solution)/shard_map/all_gather | solution.py:112
  328.6 144.0 %copy-start.4 = (f32[320,768]{1,0:T(8,128)}, f32[320,768]{1,0:T(8,128)S(1)}, u32[]{:S(2)}) copy-start(f32[320,768]{1,0:T(8,128)S(1)} %get-tuple-element.408) | copy-start | bytes 2949124
  481.0 37.2 %reduce-scatter.35.cloned.1.call-start = ((), (), s32[]{:S(2)}) async-start(), calls=%async_computation.22 | async-start | bytes 409600 | tf_op jit(solution)/shard_map/while
  499.2 39.4 %reduce-scatter.37.cloned.1.call-start = ((), (), s32[]{:S(2)}) async-start(), calls=%async_computation.23 | async-start | bytes 409600 | tf_op jit(solution)/shard_map/while
  540.2 36.6 %reduce-scatter.35.cloned.1.call-start = ((), (), s32[]{:S(2)}) async-start(), calls=%async_computation.22 | async-start | bytes 409600 | tf_op jit(solution)/shard_map/while
  558.4 38.9 %reduce-scatter.37.cloned.1.call-start = ((), (), s32[]{:S(2)}) async-start(), calls=%async_computation.23 | async-start | bytes 409600 | tf_op jit(solution)/shard_map/while
  598.9 36.6 %reduce-scatter.35.cloned.1.call-start = ((), (), s32[]{:S(2)}) async-start(), calls=%async_computation.22 | async-start | bytes 409600 | tf_op jit(solution)/shard_map/while
  617.1 39.0 %reduce-scatter.37.cloned.1.call-start = ((), (), s32[]{:S(2)}) async-start(), calls=%async_computation.23 | async-start | bytes 409600 | tf_op jit(solution)/shard_map/while
  657.7 36.6 %reduce-scatter.35.cloned.1.call-start = ((), (), s32[]{:S(2)}) async-start(), calls=%async_computation.22 | async-start | bytes 409600 | tf_op jit(solution)/shard_map/while
  675.9 38.9 %reduce-scatter.37.cloned.1.call-start = ((), (), s32[]{:S(2)}) async-start(), calls=%async_computation.23 | async-start | bytes 409600 | tf_op jit(solution)/shard_map/while
  716.4 36.6 %reduce-scatter.35.cloned.1.call-start = ((), (), s32[]{:S(2)}) async-start(), calls=%async_computation.22 | async-start | bytes 409600 | tf_op jit(solution)/shard_map/while
  734.6 38.9 %reduce-scatter.37.cloned.1.call-start = ((), (), s32[]{:S(2)}) async-start(), calls=%async_computation.23 | async-start | bytes 409600 | tf_op jit(solution)/shard_map/while
  775.1 36.6 %reduce-scatter.35.cloned.1.call-start = ((), (), s32[]{:S(2)}) async-start(), calls=%async_computation.22 | async-start | bytes 409600 | tf_op jit(solution)/shard_map/while
  793.2 38.9 %reduce-scatter.37.cloned.1.call-start = ((), (), s32[]{:S(2)}) async-start(), calls=%async_computation.23 | async-start | bytes 409600 | tf_op jit(solution)/shard_map/while
  833.8 104.1 %reduce-scatter.23.cloned.1.call-start = ((), (), s32[]{:S(2)}) async-start(), calls=%async_computation.16 | async-start | bytes 2433024 | tf_op jit(solution)/shard_map/reduce_scatter | solution.py:286
  834.5 208.1 %reduce-scatter.29.cloned.1.call-start = ((), (), s32[]{:S(2)}) async-start(), calls=%async_computation.19 | async-start | bytes 2433024
  838.6 308.0 %reduce-scatter.31.cloned.1.call-start = ((), (), s32[]{:S(2)}) async-start(), calls=%async_computation.20 | async-start | bytes 2433024
  841.5 409.7 %reduce-scatter.33.cloned.1.call-start = ((), (), s32[]{:S(2)}) async-start(), calls=%async_computation.21 | async-start | bytes 2433024
  845.4 547.1 %reduce-scatter.25.cloned.1.call-start = ((), (), s32[]{:S(2)}) async-start(), calls=%async_computation.17 | async-start | bytes 9732096 | tf_op jit(solution)/shard_map/reduce_scatter | solution.py:290
  854.0 680.3 %reduce-scatter.27.cloned.1.call-start = ((), (), s32[]{:S(2)}) async-start(), calls=%async_computation.18 | async-start | bytes 9732096 | tf_op jit(solution)/shard_map/reduce_scatter | solution.py:292
  (33 other events, 387.3 us)
Sparse Core Ops, SparseCore 0:
  11.4 56.8 all-gather.8
  71.7 53.2 all-gather.14
  128.4 53.0 all-gather.12
  183.5 42.4 all-gather.10
  228.0 42.3 all-gather.16
  273.7 52.9 all-gather.18
  330.0 62.4 all-gather.20
  395.9 62.4 all-gather.22
  499.3 18.8 reduce-scatter.34
  520.3 18.2 reduce-scatter.36
  558.5 18.2 reduce-scatter.34
  578.9 18.3 reduce-scatter.36
  617.2 18.3 reduce-scatter.34
  637.7 18.3 reduce-scatter.36
  676.0 18.2 reduce-scatter.34
  696.4 18.3 reduce-scatter.36
  734.7 18.2 reduce-scatter.34
  755.2 18.2 reduce-scatter.36
  793.4 18.2 reduce-scatter.34
  813.8 18.3 reduce-scatter.36
  840.5 97.3 reduce-scatter.22
  944.6 98.0 reduce-scatter.28
  1048.5 98.0 reduce-scatter.30
  1153.1 98.0 reduce-scatter.32
  1257.7 134.6 reduce-scatter.24
  1399.8 134.5 reduce-scatter.26
where the time goes:
time: 1550 us; the launch traced here: 1540 us
  waiting for transfers between devices  1100 us (71%)
  matrix products  168 us (11%)
  local copies, waits for them, and re-layouts  109 us (7%)
  blocking collectives  93.3 us (6%)
  other arithmetic  32.8 us (2%)
  loops' own time  20.3 us (1%)
  between operations  15.6 us (1%)
    unnamed x17, waiting for transfers between devices  314 us
    while x24, waiting for transfers between devices  167 us
    reduce_scatter x1, waiting for transfers between devices, per_device(): lax.psum_scatter(grad_w_contract, ('page', 'band'), scatter_dimension=0,...  142 us
    reduce_scatter x1, waiting for transfers between devices, per_device(): lax.psum_scatter(grad_w_expand, ('page', 'band'), scatter_dimension=0, ti...  141 us
    unnamed x3, blocking collectives  93.3 us
    all_gather x1, waiting for transfers between devices, per_device(): lax.all_gather(low_masters[9], ('page', 'band'), axis=0, tiled=True)  63.7 us
    all_gather x1, waiting for transfers between devices, per_device(): lax.all_gather(low_masters[2], ('page', 'band'), axis=0, tiled=True)  53.8 us
    all_gather x1, waiting for transfers between devices, per_device(): lax.all_gather(low_masters[11], ('page', 'band'), axis=0, tiled=True)  52.4 us
  transfers between devices with their start and end apart: 26, of which 26 were waited for; matrix products, arithmetic and copies ran while one was open for 12% of the time, Pallas kernels for 0%

commit v1 on v0

v1 whole, which is shorter than its diff:
```python
import functools
import itertools
import math

import jax
import jax.numpy as jnp
from jax import lax
from jax.experimental import pallas as pl
from jax.experimental.pallas import tpu as pltpu
from jax.sharding import PartitionSpec as P

HEAD_DIM = 64
PAIR = 2 * HEAD_DIM
EPSILON = 1e-12
AXES = ("page", "band")
SLAB = 128
TAIL = 16
BF16, F32 = jnp.bfloat16, jnp.float32
VMEM_LIMIT = 56 * 2**20


def dot(left, right):
    return lax.dot_general(left, right, (((1,), (0,)), ((), ())), preferred_element_type=F32)


def times_transposed(left, right):
    return lax.dot_general(left, right, (((1,), (1,)), ((), ())), preferred_element_type=F32)


def outer_sum(left, right):
    return lax.dot_general(left, right, (((0,), (0,)), ((), ())), preferred_element_type=F32)


class Grid:
    def __init__(self, pages, bands):
        self.side = math.isqrt(pages // 2)
        assert self.side * self.side * 2 == pages
        self.bands = bands
        self.devices = pages * bands
        self.quads = self.side * self.side

    def linear(self, i, j, c, z):
        return ((i * self.side + j) * 2 + c) * self.bands + z

    def permute(self, array, move):
        side, bands = self.side, self.bands
        pairs = []
        for i, j, c, z in itertools.product(range(side), range(side), range(2), range(bands)):
            ti, tj, tc, tz = move(i, j, c, z)
            pairs.append((self.linear(i, j, c, z), self.linear(ti % side, tj % side, tc, tz % bands)))
        return lax.ppermute(array, AXES, pairs)

    def along_z(self, array, step):
        return self.permute(array, lambda i, j, c, z: (i, j, c, z + step))

    def near(self, array, step):
        return self.permute(
            array, lambda i, j, c, z: (i, j + step, c, z) if c == 0 else (i + step, j, c, z)
        )

    def far(self, array, step):
        return self.permute(
            array, lambda i, j, c, z: (i + step, j, c, z) if c == 0 else (i, j + step, c, z)
        )

    def across(self, array):
        return self.permute(array, lambda i, j, c, z: (i, j, 1 - c, z))

    def place(self):
        page, z = lax.axis_index("page"), lax.axis_index("band")
        return page // (2 * self.side), (page // 2) % self.side, page % 2, z


def gather_rows(grid, shard):
    rows, width = shard.shape
    i, j, c, z = grid.place()
    block = jnp.zeros((grid.bands, rows, width), shard.dtype)
    for step in range(grid.bands):
        piece = shard if step == 0 else grid.along_z(shard, step)
        block = lax.dynamic_update_slice(block, piece[None], ((z - step) % grid.bands, 0, 0))
    tall = grid.bands * rows
    block = block.reshape(tall, width)
    near = [block] + [grid.near(block, step) for step in range(1, grid.side)]
    near_all = jnp.stack(near)
    far = [near_all] + [grid.far(near_all, step) for step in range(1, grid.side)]
    own = [far[a][b] for a in range(grid.side) for b in range(grid.side)]
    sent = [near_all] + far[1:]
    other = [grid.across(item) for item in sent]
    other = [other[a][b] for a in range(grid.side) for b in range(grid.side)]
    whole = jnp.zeros((grid.quads * 2, tall, width), shard.dtype)
    for core, blocks in ((c, own), (1 - c, other)):
        for a in range(grid.side):
            for b in range(grid.side):
                di = jnp.where(core == 0, a, b)
                dj = jnp.where(core == 0, b, a)
                index = (((i - di) % grid.side) * grid.side + (j - dj) % grid.side) * 2 + core
                whole = lax.dynamic_update_slice(whole, blocks[a * grid.side + b][None], (index, 0, 0))
    return whole.reshape(grid.devices * rows, width)


def relative(grid, full):
    rows = full.shape[0] // grid.devices
    i, j, c, z = grid.place()
    blocks = full.reshape(grid.quads * 2, grid.bands, rows, full.shape[1])
    cores = []
    for d in range(2):
        core = (c + d) % 2
        fars = []
        for a in range(grid.side):
            nears = []
            for b in range(grid.side):
                di = jnp.where(core == 0, a, b)
                dj = jnp.where(core == 0, b, a)
                index = (((i + di) % grid.side) * grid.side + (j + dj) % grid.side) * 2 + core
                nears.append(lax.dynamic_index_in_dim(blocks, index, 0, False))
            fars.append(nears)
        cores.append(fars)
    return cores


def scatter_sum(grid, full):
    side = grid.side
    z = lax.axis_index("band")
    keep, send = relative(grid, full)
    send = jnp.stack([jnp.stack(row) for row in send])
    got = grid.across(send)
    total = [[keep[a][b].astype(F32) + got[a, b].astype(F32) for b in range(side)] for a in range(side)]
    for a in range(1, side):
        got = grid.far(jnp.stack(total[a]).astype(BF16), a)
        for b in range(side):
            total[0][b] = total[0][b] + got[b].astype(F32)
    own = total[0][0]
    for b in range(1, side):
        own = own + grid.near(total[0][b].astype(BF16), b).astype(F32)
    result = lax.dynamic_index_in_dim(own, z, 0, False)
    for step in range(1, grid.bands):
        part = lax.dynamic_index_in_dim(own, (z + step) % grid.bands, 0, False).astype(BF16)
        result = result + grid.along_z(part, step).astype(F32)
    return result


def head_mask(rows, head):
    lanes = lax.broadcasted_iota(jnp.int32, (rows, PAIR), 1)
    return (lanes // HEAD_DIM) == head


def attend_kernel(pieces, *refs):
    hidden = refs[:pieces]
    wq, wk, wv, vec, own_doc, all_doc = refs[pieces : pieces + 6]
    q_out, k_out, v_out, att_out, log_out, bias = refs[pieces + 6 :]
    tokens = q_out.shape[0]
    keys = k_out.shape[0]

    @pl.when(pl.program_id(0) == 0)
    def _():
        bias[...] = jnp.where(own_doc[...] == all_doc[...], 0.0, -1e30).astype(F32)

    q_out[...] = (dot(hidden[0][0:tokens, :], wq[...]) + vec[0:1, :]).astype(BF16)
    for p in range(pieces):
        rows = slice(p * tokens, (p + 1) * tokens)
        part = hidden[p][0:tokens, :]
        k_out[rows, :] = dot(part, wk[...]).astype(BF16)
        v_out[rows, :] = (dot(part, wv[...]) + vec[1:2, :]).astype(BF16)
    lane = lax.broadcasted_iota(jnp.int32, (tokens, 128), 1)
    logs = jnp.zeros((tokens, 128), F32)
    ones = jnp.ones((keys, PAIR), BF16)
    for pair in range(q_out.shape[1] // PAIR):
        cols = slice(pair * PAIR, (pair + 1) * PAIR)
        query = q_out[:, cols]
        key = k_out[:, cols]
        value = jnp.concatenate([v_out[:, cols], ones], axis=1)
        outs = []
        for head in range(2):
            picked = jnp.where(head_mask(tokens, head), query * HEAD_DIM**-0.5, 0).astype(BF16)
            scores = times_transposed(picked, key) + bias[...]
            peak = jnp.max(scores, axis=1, keepdims=True)
            weights = jnp.exp(scores - peak).astype(BF16)
            both = dot(weights, value)
            outs.append(both[:, :PAIR] / both[:, PAIR:])
            total = peak + jnp.log(both[:, PAIR:])
            logs = jnp.where(lane == pair * 2 + head, total, logs)
        att_out[:, cols] = jnp.where(head_mask(tokens, 0), outs[0], outs[1]).astype(BF16)
    log_out[...] = logs[None]


def attend(hidden, weights, vec, own_doc, all_doc):
    pieces = len(hidden)
    tokens, width = hidden[0].shape
    keys = pieces * tokens
    step = 256
    groups = width // step
    column = lambda offset: pl.BlockSpec((width, step), lambda g, o=offset: (0, o * groups + g))
    whole = lambda shape: pl.BlockSpec(shape, lambda g: (0, 0))
    tall = lambda rows: pl.BlockSpec((rows, step), lambda g: (0, g))
    return pl.pallas_call(
        functools.partial(attend_kernel, pieces),
        grid=(groups,),
        in_specs=[whole(item.shape) for item in hidden]
        + [column(0), column(1), column(2), tall(8), whole(own_doc.shape), whole(all_doc.shape)],
        out_specs=[
            tall(tokens),
            tall(keys),
            tall(keys),
            tall(tokens),
            pl.BlockSpec((1, tokens, 128), lambda g: (g, 0, 0)),
        ],
        out_shape=[
            jax.ShapeDtypeStruct((tokens, width), BF16),
            jax.ShapeDtypeStruct((keys, width), BF16),
            jax.ShapeDtypeStruct((keys, width), BF16),
            jax.ShapeDtypeStruct((tokens, width), BF16),
            jax.ShapeDtypeStruct((groups, tokens, 128), F32),
        ],
        scratch_shapes=[pltpu.VMEM((tokens, keys), F32)],
        compiler_params=pltpu.CompilerParams(vmem_limit_bytes=VMEM_LIMIT),
        cost_estimate=pl.CostEstimate(
            flops=2 * keys * width * width * 3, bytes_accessed=16 * 2**20, transcendentals=0
        ),
        name="attend",
    )(*hidden, weights, weights, weights, vec, own_doc, all_doc)


def attend_back_kernel(q, k, v, grad, att, logs, own_doc, all_doc, dq_out, dk_out, dv_out, bias):
    tokens = q.shape[0]
    pair = pl.program_id(0)

    @pl.when(pair == 0)
    def _():
        bias[...] = jnp.where(own_doc[...] == all_doc[...], 0.0, -1e30).astype(F32)

    lane = lax.broadcasted_iota(jnp.int32, (tokens, 128), 1)
    key, value = k[...], v[...]
    product = grad[...].astype(F32) * att[...].astype(F32)
    dq, dk, dv = [], 0.0, 0.0
    for head in range(2):
        mask = head_mask(tokens, head)
        query = jnp.where(mask, q[...] * HEAD_DIM**-0.5, 0).astype(BF16)
        part = jnp.where(mask, grad[...], 0).astype(BF16)
        slot = (pair % 2) * 2 + head
        log_total = jnp.sum(jnp.where(lane == slot, logs[0], 0.0), axis=1, keepdims=True)
        inner = jnp.sum(jnp.where(mask, product, 0.0), axis=1, keepdims=True)
        weights = jnp.exp(times_transposed(query, key) + bias[...] - log_total)
        back = (weights * (times_transposed(part, value) - inner)).astype(BF16)
        dq.append(dot(back, key) * HEAD_DIM**-0.5)
        dk = dk + outer_sum(back, query)
        dv = dv + outer_sum(weights.astype(BF16), part)
    dq_out[...] = jnp.where(head_mask(tokens, 0), dq[0], dq[1]).astype(BF16)
    dk_out[...] = dk.astype(BF16)
    dv_out[...] = dv.astype(BF16)


def attend_back(q, k, v, grad, att, logs, own_doc, all_doc):
    tokens, width = q.shape
    keys = k.shape[0]
    short = pl.BlockSpec((tokens, PAIR), lambda g: (0, g))
    tall = pl.BlockSpec((keys, PAIR), lambda g: (0, g))
    whole = lambda shape: pl.BlockSpec(shape, lambda g: (0, 0))
    return pl.pallas_call(
        attend_back_kernel,
        grid=(width // PAIR,),
        in_specs=[
            short,
            tall,
            tall,
            short,
            short,
            pl.BlockSpec((1, tokens, 128), lambda g: (g // 2, 0, 0)),
            whole(own_doc.shape),
            whole(all_doc.shape),
        ],
        out_specs=[short, tall, tall],
        out_shape=[
            jax.ShapeDtypeStruct((tokens, width), BF16),
            jax.ShapeDtypeStruct((keys, width), BF16),
            jax.ShapeDtypeStruct((keys, width), BF16),
        ],
        scratch_shapes=[pltpu.VMEM((tokens, keys), F32)],
        compiler_params=pltpu.CompilerParams(vmem_limit_bytes=VMEM_LIMIT),
        cost_estimate=pl.CostEstimate(
            flops=2 * keys * width * width * 4, bytes_accessed=16 * 2**20, transcendentals=0
        ),
        name="attend_back",
    )(q, k, v, grad, att, logs, own_doc, all_doc)


def layer_norm(inputs, scale_gain, shift_bias):
    centred = inputs - jnp.mean(inputs, axis=-1, keepdims=True)
    variance = jnp.mean(centred * centred, axis=-1, keepdims=True)
    inverse = lax.rsqrt(variance + EPSILON)
    normed = centred * inverse
    return normed * scale_gain + shift_bias, normed, inverse


def norm_back(grad_out, normed, inverse, scale_gain):
    grad_normed = grad_out * scale_gain
    inner = (
        grad_normed
        - jnp.mean(grad_normed, axis=-1, keepdims=True)
        - normed * jnp.mean(grad_normed * normed, axis=-1, keepdims=True)
    )
    return inner * inverse, jnp.sum(grad_out * normed, axis=0), jnp.sum(grad_out, axis=0)


def per_device(
    grid,
    hidden_in,
    lengths,
    permutation,
    query_weight,
    query_bias,
    key_weight,
    value_weight,
    value_bias,
    mix_weight,
    mix_bias,
    first_gain,
    first_shift,
    expand_weight,
    expand_bias,
    contract_weight,
    contract_bias,
    second_gain,
    second_shift,
    cotangent,
):
    tokens, width = hidden_in.shape
    wide = contract_weight.shape[0] * grid.devices
    rows = query_weight.shape[0]
    bands = grid.bands

    ends = jnp.cumsum(lengths[0])
    docs = jnp.sum((permutation[0][:, None] >= ends[None, :]).astype(jnp.int32), axis=1)
    own_doc = docs.astype(F32)[:, None]
    vectors = [query_bias, value_bias, mix_bias, first_gain, first_shift, contract_bias, second_gain, second_shift]
    slab = jnp.concatenate(
        [jnp.stack(vectors, axis=1), expand_bias.reshape(rows, wide // width)], axis=1
    )
    slab = jnp.pad(slab, ((0, 0), (0, SLAB - slab.shape[1])))
    shard_a = jnp.concatenate([query_weight, key_weight, value_weight, slab], axis=1).astype(BF16)
    shard_b = jnp.concatenate([mix_weight, expand_weight], axis=1).astype(BF16)
    shard_c = contract_weight.astype(BF16)
    marks = jnp.pad(docs.astype(BF16)[None], ((0, TAIL - 1), (0, width - tokens)))
    message = jnp.concatenate([hidden_in, marks])

    full_a = gather_rows(grid, shard_a)
    others = [grid.along_z(message, step) for step in range(1, bands)]
    full_b = gather_rows(grid, shard_b)
    full_c = gather_rows(grid, shard_c)

    hidden = [hidden_in] + [item[:tokens] for item in others]
    all_doc = jnp.concatenate(
        [docs.astype(F32)[None]] + [item[tokens : tokens + 1, :tokens].astype(F32) for item in others], axis=1
    )
    slabs = full_a[:, 3 * width :].astype(F32)
    vec = jnp.transpose(slabs[:, :8])
    b_expand = slabs[:, 8 : 8 + wide // width].reshape(wide)

    q, k, v, attended, logs = attend(hidden, full_a, vec, own_doc, all_doc)

    w_mix, w_expand = full_b[:, :width], full_b[:, width:]
    _, _, b_mix, gain_one, shift_one, b_contract, gain_two, shift_two = [vec[n] for n in range(8)]
    first, first_normed, first_inverse = layer_norm(
        hidden_in.astype(F32) + (dot(attended, w_mix) + b_mix), gain_one, shift_one
    )
    first_low = first.astype(BF16)
    expanded = dot(first_low, w_expand) + b_expand
    chance = 0.5 * (1.0 + lax.erf(expanded * (0.5**0.5)))
    density = jnp.exp(-0.5 * expanded * expanded) * ((2.0 * math.pi) ** -0.5)
    activated = (expanded * chance).astype(BF16)
    slope = chance + expanded * density
    contracted = dot(activated, full_c) + b_contract
    result, second_normed, second_inverse = layer_norm(first + contracted, gain_two, shift_two)
    grad_second, d_gain_two, d_shift_two = norm_back(
        cotangent.astype(F32), second_normed, second_inverse, gain_two
    )
    contract_low = grad_second.astype(BF16)
    d_contract = scatter_sum(grid, outer_sum(activated, contract_low).astype(BF16))
    d_b_contract = jnp.sum(contract_low.astype(F32), axis=0)
    expanded_low = (times_transposed(contract_low, full_c) * slope).astype(BF16)
    d_b_expand = jnp.sum(expanded_low.astype(F32), axis=0)
    grad_first = grad_second + times_transposed(expanded_low, w_expand)
    grad_first_sum, d_gain_one, d_shift_one = norm_back(grad_first, first_normed, first_inverse, gain_one)
    mixed_low = grad_first_sum.astype(BF16)
    d_b_mix = jnp.sum(mixed_low.astype(F32), axis=0)
    d_b = jnp.concatenate([outer_sum(attended, mixed_low), outer_sum(first_low, expanded_low)], axis=1)
    d_b = scatter_sum(grid, d_b.astype(BF16))
    attended_back = times_transposed(mixed_low, w_mix).astype(BF16)

    dq, dk, dv = attend_back(q, k, v, attended_back, attended, logs, own_doc, all_doc)
    w_query, w_key, w_value = [full_a[:, n * width : (n + 1) * width] for n in range(3)]
    back = times_transposed(dk, w_key) + times_transposed(dv, w_value)
    grad_input = grad_first_sum + times_transposed(dq, w_query) + back[:tokens]
    for step in range(1, bands):
        part = back[step * tokens : (step + 1) * tokens].astype(BF16)
        grad_input = grad_input + grid.along_z(part, -step).astype(F32)

    every = jnp.concatenate(hidden)
    column = lambda item: jnp.sum(item.astype(F32), axis=0)
    d_vec = jnp.stack(
        [column(dq), column(dv), d_b_mix, d_gain_one, d_shift_one, d_b_contract, d_gain_two, d_shift_two]
    )
    d_slab = jnp.concatenate([jnp.transpose(d_vec), d_b_expand.reshape(width, wide // width)], axis=1)
    d_slab = jnp.pad(d_slab, ((0, 0), (0, SLAB - d_slab.shape[1])))
    d_a = jnp.concatenate(
        [
            outer_sum(hidden_in, dq),
            outer_sum(every, dk),
            outer_sum(every, dv),
            d_slab,
        ],
        axis=1,
    )
    d_a = scatter_sum(grid, d_a.astype(BF16))
    slab = d_a[:, 3 * width :]
    small = [slab[:, n] for n in range(8)]
    return (
        result.astype(BF16),
        grad_input.astype(BF16),
        d_a[:, :width],
        small[0],
        d_a[:, width : 2 * width],
        d_a[:, 2 * width : 3 * width],
        small[1],
        d_b[:, :width],
        small[2],
        small[3],
        small[4],
        d_b[:, width:],
        slab[:, 8 : 8 + wide // width].reshape(-1),
        d_contract,
        small[5],
        small[6],
        small[7],
    )


def solution(mesh):
    grid = Grid(mesh.shape["page"], mesh.shape["band"])
    matrix, vector = P(AXES, None), P(AXES)
    parameters = (
        matrix,
        vector,
        matrix,
        matrix,
        vector,
        matrix,
        vector,
        vector,
        vector,
        matrix,
        vector,
        matrix,
        vector,
        vector,
        vector,
    )
    return jax.shard_map(
        functools.partial(per_device, grid),
        mesh=mesh,
        in_specs=(matrix, P("page", None), P("page", "band")) + parameters + (matrix,),
        out_specs=(matrix, matrix) + parameters,
        check_vma=False,
    )
```

time: 1550 us -> 383 us (0.25)
  waiting for transfers between devices: 1100 us -> 125 us
  matrix products: 168 us -> 55.6 us
  blocking collectives: 93.3 us -> 0 us
  starting transfers between devices: 1.08 us -> 68.7 us
  local copies, waits for them, and re-layouts: 109 us -> 60.2 us
  Pallas kernels: 0 us -> 33.9 us
  loops' own time: 20.3 us -> 0 us
    unnamed x17 -> x0, waiting for transfers between devices: 314 us -> none
    all_gather x8 -> x0, waiting for transfers between devices: 312 us -> none  [the longest x1 63.7 us: per_device(): lax.all_gather(low_masters[9], ('page', 'band'), axis=0, tiled=True)]
    reduce_scatter x3 -> x0, waiting for transfers between devices: 307 us -> none  [the longest x1 142 us: per_device(): lax.psum_scatter(grad_w_contract, ('page', 'band'), scatter_dimension=0,...]
    while x24 -> x0, waiting for transfers between devices: 167 us -> none
    ppermute x0 -> x45, waiting for transfers between devices: none -> 125 us  [permute(): return lax.ppermute(array, AXES, pairs)]
    dot_general x48 -> x3, matrix products: 133 us -> 10.7 us  [dot(): lax.dot_general(left, right, (((1,), (0,)), ((), ())), preferred_element_...]
    unnamed x3 -> x0, blocking collectives: 93.3 us -> none
    ppermute x0 -> x45, starting transfers between devices: none -> 68.7 us  [permute(): return lax.ppermute(array, AXES, pairs)]
  transfers between devices with their start and end apart: 26 -> 45, of which waited for: 26 -> 16; matrix products, arithmetic and copies ran while one was open for 12% -> 20% of each run, Pallas kernels for 0% -> 4%
where the time goes in v1:
time: 383 us; the launch traced here: 376 us
  waiting for transfers between devices  125 us (33%)
  starting transfers between devices  68.7 us (18%)
  local copies, waits for them, and re-layouts  60.2 us (16%)
  matrix products  55.6 us (15%)
  Pallas kernels  33.9 us (9%)
  other arithmetic  30.9 us (8%)
    ppermute x45, waiting for transfers between devices, permute(): return lax.ppermute(array, AXES, pairs)  125 us
    ppermute x45, starting transfers between devices, permute(): return lax.ppermute(array, AXES, pairs)  68.7 us
    dynamic_update_slice x24, local copies, waits for them, and re-layouts, gather_rows(): lax.dynamic_update_slice(whole, blocks[a * grid.side + b][None], (index,...  26.3 us
    dot_general x6, matrix products, outer_sum(): lax.dot_general(left, right, (((0,), (0,)), ((), ())), preferred_element_...  23.3 us
    dot_general x6, matrix products, times_transposed(): lax.dot_general(left, right, (((1,), (1,)), ((), ())), preferred_element_...  21.5 us
    pallas_call x1, Pallas kernels, attend_back(): pl.pallas_call(attend_back_kernel, grid=(width // PAIR,), in_specs=[short...  18.6 us
    pallas_call x1, Pallas kernels, attend(): pl.pallas_call(functools.partial(attend_kernel, pieces), grid=(groups,),...  15.3 us
    dot_general x3, matrix products, dot(): lax.dot_general(left, right, (((1,), (0,)), ((), ())), preferred_element_...  10.7 us
  transfers between devices with their start and end apart: 45, of which 16 were waited for; matrix products, arithmetic and copies ran while one was open for 20% of the time, Pallas kernels for 4%

profile of v1, /device:TPU:0, one launch (start us, length us, event | category | flops | bytes accessed | tf_op | source)
XLA Modules:
  0.0 376.3 jit_solution(8212075502978538646)
XLA Ops:
  10.3 5.1 %collective-permute-start.5 = (bf16[24,2432]{1,0:T(8,128)(2,1)S(1)}, bf16[24,2432]{1,0:T(8,128)(2,1)S(1)}, u32[]{:S(2)}, u32[]{:S(2)}) collective-permute-start(bf16[24,2432]{1,0:T(8,128)(2,1)S(1)} %pad_maximum_fusion.14), channel_id=1, source_target_pairs={{0,3},{1,0},{2,1},{3,2},{4,7},{5,4},{6,5},{7,6},{8,11},{9,8},{10,9... | collective-permute-start | bytes 350216 | tf_op jit(solution)/shard_map/ppermute | solution.py:51
  25.0 9.9 %collective-permute-start.10 = (bf16[24,3840]{1,0:T(8,128)(2,1)S(1)}, bf16[24,3840]{1,0:T(8,128)(2,1)S(1)}, u32[]{:S(2)}, u32[]{:S(2)}) collective-permute-start(bf16[24,3840]{1,0:T(8,128)(2,1)S(1)} %pad_maximum_fusion.13), channel_id=1, source_target_pairs={{0,1},{1,2},{2,3},{3,0},{4,5},{5,6},{6,7},{7,4},{8,9},{9,10},{10,1... | collective-permute-start | bytes 552968 | tf_op jit(solution)/shard_map/ppermute | solution.py:51
  40.5 4.4 %collective-permute-done.17 = bf16[96,768]{1,0:T(8,128)(2,1)S(1)} collective-permute-done((bf16[96,768]{1,0:T(8,128)(2,1)S(1)}, bf16[96,768]{1,0:T(8,128)(2,1)S(1)}, u32[]{:S(2)}, u32[]{:S(2)}) %collective-permute-start.17) | collective-permute-done | bytes 147488 | tf_op jit(solution)/shard_map/ppermute | solution.py:51
  44.9 3.6 collective-permute-start.19
  50.9 7.2 %collective-permute-start.2 = (bf16[336,768]{1,0:T(8,128)(2,1)S(1)}, bf16[336,768]{1,0:T(8,128)(2,1)S(1)}, u32[]{:S(2)}, u32[]{:S(2)}) collective-permute-start(bf16[336,768]{1,0:T(8,128)(2,1)S(1)} %fusion.57), channel_id=1, source_target_pairs={{0,3},{1,0},{2,1},{3,2},{4,7},{5,4},{6,5},{7,6},{8,11},{9,8},{10,9... | collective-permute-start | bytes 1548296 | tf_op jit(solution)/shard_map/ppermute | solution.py:51
  59.4 3.9 %collective-permute-start.1 = (bf16[336,768]{1,0:T(8,128)(2,1)S(1)}, bf16[336,768]{1,0:T(8,128)(2,1)S(1)}, u32[]{:S(2)}, u32[]{:S(2)}) collective-permute-start(bf16[336,768]{1,0:T(8,128)(2,1)S(1)} %fusion.57), channel_id=1, source_target_pairs={{0,2},{1,3},{2,0},{3,1},{4,6},{5,7},{6,4},{7,5},{8,10},{9,11},{10,... | collective-permute-start | bytes 1548296 | tf_op jit(solution)/shard_map/ppermute | solution.py:51
  74.3 29.7 %collective-permute-done.1 = bf16[336,768]{1,0:T(8,128)(2,1)S(1)} collective-permute-done((bf16[336,768]{1,0:T(8,128)(2,1)S(1)}, bf16[336,768]{1,0:T(8,128)(2,1)S(1)}, u32[]{:S(2)}, u32[]{:S(2)}) %collective-permute-start.1) | collective-permute-done | bytes 516128 | tf_op jit(solution)/shard_map/ppermute | solution.py:51
  120.4 6.3 %collective-permute-done.7 = bf16[2,96,2432]{2,1,0:T(8,128)(2,1)S(1)} collective-permute-done((bf16[2,96,2432]{2,1,0:T(8,128)(2,1)S(1)}, bf16[2,96,2432]{2,1,0:T(8,128)(2,1)S(1)}, u32[]{:S(2)}, u32[]{:S(2)}) %collective-permute-start.7) | collective-permute-done | bytes 933920 | tf_op jit(solution)/shard_map/ppermute | solution.py:51
  131.5 8.0 %collective-permute-done.21 = bf16[2,384,768]{2,1,0:T(8,128)(2,1)} collective-permute-done((bf16[2,384,768]{2,1,0:T(8,128)(2,1)S(1)}, bf16[2,384,768]{2,1,0:T(8,128)(2,1)}, u32[]{:S(2)}, u32[]{:S(2)}) %collective-permute-start.21) | collective-permute-done | bytes 1179680 | tf_op jit(solution)/shard_map/ppermute | solution.py:51
  145.1 10.0 %collective-permute-done.14 = bf16[2,96,3840]{2,1,0:T(8,128)(2,1)S(1)} collective-permute-done((bf16[2,96,3840]{2,1,0:T(8,128)(2,1)S(1)}, bf16[2,96,3840]{2,1,0:T(8,128)(2,1)S(1)}, u32[]{:S(2)}, u32[]{:S(2)}) %collective-permute-start.14) | collective-permute-done | bytes 1474592 | tf_op jit(solution)/shard_map/ppermute | solution.py:51
  164.2 15.3 %attend.1 = (bf16[320,768]{1,0:T(8,128)(2,1)}, bf16[1280,768]{1,0:T(8,128)(2,1)}, bf16[1280,768]{1,0:T(8,128)(2,1)}, bf16[320,768]{1,0:T(8,128)(2,1)}, f32[3,320,128]{2,1,0:T(8,128)}) custom-call(bf16[320,768]{1,0:T(8,128)(2,1)} %refs_0_.1, bf16[320,768]{1,0:T(8,128)(2,1)} %slice.309.refs_1_, bf16[320,768]{1,0:T(8,128)(2,1)} %slice.310.refs_2_, ...), custom_call_target="tpu_custom_call" | custom-call | flops 4529848320 | bytes 16777216 | tf_op jit(solution)/shard_map/attend/pallas_call | solution.py:195
  187.5 3.9 %multiply_convert_fusion = (bf16[320,3072]{1,0:T(8,128)(2,1)S(1)}, f32[320,3072]{1,0:T(8,128)S(1)}) fusion(f32[3072]{0:T(1024)S(1)} %add.831, bf16[768,3840]{1,0:T(8,128)(2,1)} %bitcast.29, f32[320,768]{1,0:T(8,128)S(1)} %get-tuple-element.98, f32[768]{0:T(1024)S(1)} %get-tuple-element.51, f32[768]{0:T(1024)S(1)} %get-tuple-element.52, ...), kind=kOutput, calls=%fused_computation.30 | convolution fusion | flops 1517076480 | bytes 11620864 | tf_op jit(solution)/shard_map/dot_general | solution.py:23
  191.5 4.9 %fusion.86 = (f32[320]{0:T(512)S(1)}, f32[320,768]{1,0:T(8,128)S(1)}) fusion(f32[768]{0:T(1024)S(1)} %get-tuple-element.50, bf16[320,3072]{1,0:T(8,128)(2,1)S(1)} %get-tuple-element.99, bf16[3072,768]{1,0:T(8,128)(2,1)} %bitcast.37, f32[768]{0:T(1024)S(1)} %get-tuple-element.51, f32[768]{0:T(1024)S(1)} %get-tuple-element.52, f32[320]{0:T(512)S(1)} %add_rsqrt_fusion.1, ...), kind=kOutput, calls=%fused_computation.265 | convolution fusion | flops 1511669504 | bytes 8663808 | tf_op jit(solution)/shard_map/dot_general | solution.py:23
  198.4 5.0 %fusion.88 = (bf16[3072]{0:T(1024)(128)(2,1)S(1)}, bf16[320,3072]{1,0:T(8,128)(2,1)S(1)}) fusion(f32[320,3072]{1,0:T(8,128)S(1)} %get-tuple-element.100, bf16[3072,768]{1,0:T(8,128)(2,1)} %bitcast.37, f32[320,768]{1,0:T(8,128)S(1)} %get-tuple-element.55), kind=kOutput, calls=%fused_computation.267 | convolution fusion | flops 1521005568 | bytes 11606016 | tf_op jit(solution)/shard_map/dot_general | solution.py:27
  203.4 5.1 %multiply_reduce_fusion = (bf16[768]{0:T(1024)(128)(2,1)S(1)}, f32[320]{0:T(512)S(1)}, f32[320]{0:T(512)S(1)}, bf16[768]{0:T(1024)(128)(2,1)S(1)}, f32[320,768]{1,0:T(8,128)S(1)}) fusion(f32[320,768]{1,0:T(8,128)S(1)} %get-tuple-element.98, f32[320]{0:T(512)S(1)} %add_rsqrt_fusion.1, f32[320]{0:T(512)S(1)} %broadcast_multiply_fusion.5, ...), kind=kOutput, calls=%fused_computation.99 | convolution fusion | flops 1512404992 | bytes 9645056 | tf_op jit(solution)/shard_map/dot_general | solution.py:27
  212.4 18.6 %attend_back.1 = (bf16[320,768]{1,0:T(8,128)(2,1)}, bf16[1280,768]{1,0:T(8,128)(2,1)}, bf16[1280,768]{1,0:T(8,128)(2,1)}) custom-call(bf16[320,768]{1,0:T(8,128)(2,1)} %get-tuple-element.26.q, bf16[1280,768]{1,0:T(8,128)(2,1)} %get-tuple-element.27.k, bf16[1280,768]{1,0:T(8,128)(2,1)} %get-tuple-element.28.v, ...), custom_call_target="tpu_custom_call" | custom-call | flops 6039797760 | bytes 16777216 | tf_op jit(solution)/shard_map/attend_back/pallas_call | solution.py:258
  232.9 4.9 %convolution_convert_fusion.4 = bf16[768,768]{1,0:T(8,128)(2,1)} fusion(bf16[1280,768]{1,0:T(8,128)(2,1)} %get-tuple-element.32, bf16[320,768]{1,0:T(8,128)(2,1)} %slice.311.refs_3_, bf16[320,768]{1,0:T(8,128)(2,1)} %slice.310.refs_2_, bf16[320,768]{1,0:T(8,128)(2,1)} %slice.309.refs_1_, bf16[320,768]{1,0:T(8,128)(2,1)} %refs_0_.1), kind=kOutput, calls=%fused_computation.40 | convolution fusion | flops 1518403584 | bytes 5111808 | tf_op jit(solution)/shard_map/dot_general | solution.py:31
  238.9 3.0 convolution_convert_fusion.3
  242.0 6.3 %convolution_convert_fusion.1 = bf16[768,3072]{1,0:T(8,128)(2,1)} fusion(bf16[320,3072]{1,0:T(8,128)(2,1)} %copy-done.29, f32[320,768]{1,0:T(8,128)S(1)} %get-tuple-element.98, f32[768]{0:T(1024)S(1)} %get-tuple-element.51, f32[768]{0:T(1024)S(1)} %get-tuple-element.52, f32[320]{0:T(512)S(1)} %add_rsqrt_fusion.1, f32[320]{0:T(512)S(1)} %broadcast_multiply_fusion.5), kind=kOutput, calls=%fused_computation.18 | convolution fusion | flops 1513537536 | bytes 7676416 | tf_op jit(solution)/shard_map/dot_general | solution.py:31
  248.2 4.5 %convolution_convert_fusion = bf16[3072,768]{1,0:T(8,128)(2,1)} fusion(bf16[320,3072]{1,0:T(8,128)(2,1)S(1)} %copy-done.28, f32[320,768]{1,0:T(8,128)S(1)} %copy-done.10), kind=kOutput, calls=%fused_computation.17 | convolution fusion | flops 1512554496 | bytes 7667712 | tf_op jit(solution)/shard_map/dot_general | solution.py:31
  253.8 3.7 convolution_convert_fusion.5
  271.3 3.0 fusion.87
  277.9 5.7 %collective-permute-done.28 = bf16[2,4,24,2432]{3,2,1,0:T(8,128)(2,1)S(1)} collective-permute-done((bf16[2,4,24,2432]{3,2,1,0:T(8,128)(2,1)}, bf16[2,4,24,2432]{3,2,1,0:T(8,128)(2,1)S(1)}, u32[]{:S(2)}, u32[]{:S(2)}) %collective-permute-start.28) | collective-permute-done | bytes 933920 | tf_op jit(solution)/shard_map/ppermute | solution.py:51
  289.5 10.5 %collective-permute-done.29 = bf16[4,24,2432]{2,1,0:T(8,128)(2,1)S(1)} collective-permute-done((bf16[4,24,2432]{2,1,0:T(8,128)(2,1)S(1)}, bf16[4,24,2432]{2,1,0:T(8,128)(2,1)S(1)}, u32[]{:S(2)}, u32[]{:S(2)}) %collective-permute-start.29) | collective-permute-done | bytes 466976 | tf_op jit(solution)/shard_map/ppermute | solution.py:51
  301.9 4.1 %collective-permute-start.32 = (bf16[24,2432]{1,0:T(8,128)(2,1)S(1)}, bf16[24,2432]{1,0:T(8,128)(2,1)S(1)}, u32[]{:S(2)}, u32[]{:S(2)}) collective-permute-start(bf16[24,2432]{1,0:T(8,128)(2,1)S(1)} %get-tuple-element.89), channel_id=1, source_target_pairs={{0,3},{1,0},{2,1},{3,2},{4,7},{5,4},{6,5},{7,6},{8,11},{9,8},{10,9... | collective-permute-start | bytes 350216 | tf_op jit(solution)/shard_map/ppermute | solution.py:51
  306.0 14.6 %collective-permute-done.25 = bf16[320,768]{1,0:T(8,128)(2,1)S(1)} collective-permute-done((bf16[320,768]{1,0:T(8,128)(2,1)S(1)}, bf16[320,768]{1,0:T(8,128)(2,1)S(1)}, u32[]{:S(2)}, u32[]{:S(2)}) %collective-permute-start.25) | collective-permute-done | bytes 491552 | tf_op jit(solution)/shard_map/ppermute | solution.py:51
  323.3 5.3 %collective-permute-done.31 = bf16[24,2432]{1,0:T(8,128)(2,1)S(1)} collective-permute-done((bf16[24,2432]{1,0:T(8,128)(2,1)S(1)}, bf16[24,2432]{1,0:T(8,128)(2,1)S(1)}, u32[]{:S(2)}, u32[]{:S(2)}) %collective-permute-start.31) | collective-permute-done | bytes 116768 | tf_op jit(solution)/shard_map/ppermute | solution.py:51
  336.7 4.5 %collective-permute-done.41 = bf16[4,96,768]{2,1,0:T(8,128)(2,1)S(1)} collective-permute-done((bf16[4,96,768]{2,1,0:T(8,128)(2,1)S(1)}, bf16[4,96,768]{2,1,0:T(8,128)(2,1)S(1)}, u32[]{:S(2)}, u32[]{:S(2)}) %collective-permute-start.41) | collective-permute-done | bytes 589856 | tf_op jit(solution)/shard_map/ppermute | solution.py:51
  343.0 3.8 %collective-permute-start.44 = (bf16[96,768]{1,0:T(8,128)(2,1)S(1)}, bf16[96,768]{1,0:T(8,128)(2,1)S(1)}, u32[]{:S(2)}, u32[]{:S(2)}) collective-permute-start(bf16[96,768]{1,0:T(8,128)(2,1)S(1)} %get-tuple-element.85), channel_id=1, source_target_pairs={{0,3},{1,0},{2,1},{3,2},{4,7},{5,4},{6,5},{7,6},{8,11},{9,8},{10,9... | collective-permute-start | bytes 442376 | tf_op jit(solution)/shard_map/ppermute | solution.py:51
  351.0 3.8 %collective-permute-start.38 = (bf16[24,3840]{1,0:T(8,128)(2,1)S(1)}, bf16[24,3840]{1,0:T(8,128)(2,1)S(1)}, u32[]{:S(2)}, u32[]{:S(2)}) collective-permute-start(bf16[24,3840]{1,0:T(8,128)(2,1)S(1)} %get-tuple-element.82), channel_id=1, source_target_pairs={{0,3},{1,0},{2,1},{3,2},{4,7},{5,4},{6,5},{7,6},{8,11},{9,8},{10,9... | collective-permute-start | bytes 552968 | tf_op jit(solution)/shard_map/ppermute | solution.py:51
  354.8 9.5 %collective-permute-done.43 = bf16[96,768]{1,0:T(8,128)(2,1)S(1)} collective-permute-done((bf16[96,768]{1,0:T(8,128)(2,1)S(1)}, bf16[96,768]{1,0:T(8,128)(2,1)S(1)}, u32[]{:S(2)}, u32[]{:S(2)}) %collective-permute-start.43) | collective-permute-done | bytes 147488 | tf_op jit(solution)/shard_map/ppermute | solution.py:51
  365.1 9.3 %collective-permute-done.37 = bf16[24,3840]{1,0:T(8,128)(2,1)S(1)} collective-permute-done((bf16[24,3840]{1,0:T(8,128)(2,1)S(1)}, bf16[24,3840]{1,0:T(8,128)(2,1)S(1)}, u32[]{:S(2)}, u32[]{:S(2)}) %collective-permute-start.37) | collective-permute-done | bytes 184352 | tf_op jit(solution)/shard_map/ppermute | solution.py:51
  (310 shorter events, 136.6 us)
Async XLA Ops:
  10.3 26.6 %collective-permute-start.5 = (bf16[24,2432]{1,0:T(8,128)(2,1)S(1)}, bf16[24,2432]{1,0:T(8,128)(2,1)S(1)}, u32[]{:S(2)}, u32[]{:S(2)}) collective-permute-start(bf16[24,2432]{1,0:T(8,128)(2,1)S(1)} %pad_maximum_fusion.14), channel_id=1, source_target_pairs={{0,3},{1,0},{2,1},{3,2},{4,7},{5,4},{6,5},{7,6},{8,11},{9,8},{10,9... | collective-permute-start | bytes 350216 | tf_op jit(solution)/shard_map/ppermute | solution.py:51
  15.4 19.5 %collective-permute-start.4 = (bf16[24,2432]{1,0:T(8,128)(2,1)S(1)}, bf16[24,2432]{1,0:T(8,128)(2,1)S(1)}, u32[]{:S(2)}, u32[]{:S(2)}) collective-permute-start(bf16[24,2432]{1,0:T(8,128)(2,1)S(1)} %pad_maximum_fusion.14), channel_id=1, source_target_pairs={{0,2},{1,3},{2,0},{3,1},{4,6},{5,7},{6,4},{7,5},{8,10},{9,11},{10,... | collective-permute-start | bytes 350216 | tf_op jit(solution)/shard_map/ppermute | solution.py:51
  18.3 50.0 %collective-permute-start.12 = (bf16[24,3840]{1,0:T(8,128)(2,1)S(1)}, bf16[24,3840]{1,0:T(8,128)(2,1)S(1)}, u32[]{:S(2)}, u32[]{:S(2)}) collective-permute-start(bf16[24,3840]{1,0:T(8,128)(2,1)S(1)} %pad_maximum_fusion.13), channel_id=1, source_target_pairs={{0,3},{1,0},{2,1},{3,2},{4,7},{5,4},{6,5},{7,6},{8,11},{9,8},{10,9... | collective-permute-start | bytes 552968 | tf_op jit(solution)/shard_map/ppermute | solution.py:51
  21.2 45.5 %collective-permute-start.11 = (bf16[24,3840]{1,0:T(8,128)(2,1)S(1)}, bf16[24,3840]{1,0:T(8,128)(2,1)S(1)}, u32[]{:S(2)}, u32[]{:S(2)}) collective-permute-start(bf16[24,3840]{1,0:T(8,128)(2,1)S(1)} %pad_maximum_fusion.13), channel_id=1, source_target_pairs={{0,2},{1,3},{2,0},{3,1},{4,6},{5,7},{6,4},{7,5},{8,10},{9,11},{10,... | collective-permute-start | bytes 552968 | tf_op jit(solution)/shard_map/ppermute | solution.py:51
  25.0 41.7 %collective-permute-start.10 = (bf16[24,3840]{1,0:T(8,128)(2,1)S(1)}, bf16[24,3840]{1,0:T(8,128)(2,1)S(1)}, u32[]{:S(2)}, u32[]{:S(2)}) collective-permute-start(bf16[24,3840]{1,0:T(8,128)(2,1)S(1)} %pad_maximum_fusion.13), channel_id=1, source_target_pairs={{0,1},{1,2},{2,3},{3,0},{4,5},{5,6},{6,7},{7,4},{8,9},{9,10},{10,1... | collective-permute-start | bytes 552968 | tf_op jit(solution)/shard_map/ppermute | solution.py:51
  34.9 16.0 %collective-permute-start.18 = (bf16[96,768]{1,0:T(8,128)(2,1)S(1)}, bf16[96,768]{1,0:T(8,128)(2,1)S(1)}, u32[]{:S(2)}, u32[]{:S(2)}) collective-permute-start(bf16[96,768]{1,0:T(8,128)(2,1)S(1)} %get-tuple-element.59), channel_id=1, source_target_pairs={{0,2},{1,3},{2,0},{3,1},{4,6},{5,7},{6,4},{7,5},{8,10},{9,11},{10,... | collective-permute-start | bytes 442376 | tf_op jit(solution)/shard_map/ppermute | solution.py:51
  44.9 14.5 %collective-permute-start.19 = (bf16[96,768]{1,0:T(8,128)(2,1)S(1)}, bf16[96,768]{1,0:T(8,128)(2,1)S(1)}, u32[]{:S(2)}, u32[]{:S(2)}) collective-permute-start(bf16[96,768]{1,0:T(8,128)(2,1)S(1)} %get-tuple-element.59), channel_id=1, source_target_pairs={{0,3},{1,0},{2,1},{3,2},{4,7},{5,4},{6,5},{7,6},{8,11},{9,8},{10,9... | collective-permute-start | bytes 442376 | tf_op jit(solution)/shard_map/ppermute | solution.py:51
  50.9 21.9 %collective-permute-start.2 = (bf16[336,768]{1,0:T(8,128)(2,1)S(1)}, bf16[336,768]{1,0:T(8,128)(2,1)S(1)}, u32[]{:S(2)}, u32[]{:S(2)}) collective-permute-start(bf16[336,768]{1,0:T(8,128)(2,1)S(1)} %fusion.57), channel_id=1, source_target_pairs={{0,3},{1,0},{2,1},{3,2},{4,7},{5,4},{6,5},{7,6},{8,11},{9,8},{10,9... | collective-permute-start | bytes 1548296 | tf_op jit(solution)/shard_map/ppermute | solution.py:51
  59.4 44.6 %collective-permute-start.1 = (bf16[336,768]{1,0:T(8,128)(2,1)S(1)}, bf16[336,768]{1,0:T(8,128)(2,1)S(1)}, u32[]{:S(2)}, u32[]{:S(2)}) collective-permute-start(bf16[336,768]{1,0:T(8,128)(2,1)S(1)} %fusion.57), channel_id=1, source_target_pairs={{0,2},{1,3},{2,0},{3,1},{4,6},{5,7},{6,4},{7,5},{8,10},{9,11},{10,... | collective-permute-start | bytes 1548296 | tf_op jit(solution)/shard_map/ppermute | solution.py:51
  66.7 37.3 %collective-permute-start = (bf16[336,768]{1,0:T(8,128)(2,1)S(1)}, bf16[336,768]{1,0:T(8,128)(2,1)S(1)}, u32[]{:S(2)}, u32[]{:S(2)}) collective-permute-start(bf16[336,768]{1,0:T(8,128)(2,1)S(1)} %fusion.57), channel_id=1, source_target_pairs={{0,1},{1,2},{2,3},{3,0},{4,5},{5,6},{6,7},{7,4},{8,9},{9,10},{10,1... | collective-permute-start | bytes 1548296 | tf_op jit(solution)/shard_map/ppermute | solution.py:51
  66.7 45.2 %collective-permute-start.6 = (bf16[96,2432]{1,0:T(8,128)(2,1)S(1)}, bf16[96,2432]{1,0:T(8,128)(2,1)}, u32[]{:S(2)}, u32[]{:S(2)}) collective-permute-start(bf16[96,2432]{1,0:T(8,128)(2,1)S(1)} %bitcast.270), channel_id=1, source_target_pairs={{0,8},{1,9},{2,10},{3,11},{4,20},{5,21},{6,22},{7,23},{8,0},{9,1},... | collective-permute-start | bytes 1400840 | tf_op jit(solution)/shard_map/ppermute | solution.py:51
  68.3 48.2 %collective-permute-start.20 = (bf16[384,768]{1,0:T(8,128)(2,1)S(1)}, bf16[384,768]{1,0:T(8,128)(2,1)S(1)}, u32[]{:S(2)}, u32[]{:S(2)}) collective-permute-start(bf16[384,768]{1,0:T(8,128)(2,1)S(1)} %bitcast.261), channel_id=1, source_target_pairs={{0,8},{1,9},{2,10},{3,11},{4,20},{5,21},{6,22},{7,23},{8,0},{9,1},... | collective-permute-start | bytes 1769480 | tf_op jit(solution)/shard_map/ppermute | solution.py:51
  72.8 46.4 %collective-permute-start.13 = (bf16[96,3840]{1,0:T(8,128)(2,1)S(1)}, bf16[96,3840]{1,0:T(8,128)(2,1)S(1)}, u32[]{:S(2)}, u32[]{:S(2)}) collective-permute-start(bf16[96,3840]{1,0:T(8,128)(2,1)S(1)} %bitcast.258), channel_id=1, source_target_pairs={{0,8},{1,9},{2,10},{3,11},{4,20},{5,21},{6,22},{7,23},{8,0},{9,1},... | collective-permute-start | bytes 2211848 | tf_op jit(solution)/shard_map/ppermute | solution.py:51
  113.0 16.9 %collective-permute-start.8 = (bf16[2,96,2432]{2,1,0:T(8,128)(2,1)S(1)}, bf16[2,96,2432]{2,1,0:T(8,128)(2,1)S(1)}, u32[]{:S(2)}, u32[]{:S(2)}) collective-permute-start(bf16[2,96,2432]{2,1,0:T(8,128)(2,1)S(1)} %pad_maximum_fusion.9), channel_id=1, source_target_pairs={{0,4},{1,5},{2,6},{3,7},{4,0},{5,1},{6,2},{7,3},{8,12},{9,13},{10,... | collective-permute-start | bytes 2801672 | tf_op jit(solution)/shard_map/ppermute | solution.py:51
  116.6 26.7 %collective-permute-start.22 = (bf16[2,384,768]{2,1,0:T(8,128)(2,1)S(1)}, bf16[2,384,768]{2,1,0:T(8,128)(2,1)S(1)}, u32[]{:S(2)}, u32[]{:S(2)}) collective-permute-start(bf16[2,384,768]{2,1,0:T(8,128)(2,1)S(1)} %pad_maximum_fusion.7), channel_id=1, source_target_pairs={{0,4},{1,5},{2,6},{3,7},{4,0},{5,1},{6,2},{7,3},{8,12},{9,13},{10,... | collective-permute-start | bytes 3538952 | tf_op jit(solution)/shard_map/ppermute | solution.py:51
  116.8 22.7 %collective-permute-start.21 = (bf16[2,384,768]{2,1,0:T(8,128)(2,1)S(1)}, bf16[2,384,768]{2,1,0:T(8,128)(2,1)}, u32[]{:S(2)}, u32[]{:S(2)}) collective-permute-start(bf16[2,384,768]{2,1,0:T(8,128)(2,1)S(1)} %pad_maximum_fusion.7), channel_id=1, source_target_pairs={{0,16},{1,17},{2,18},{3,19},{4,12},{5,13},{6,14},{7,15},{8,24},{9,... | collective-permute-start | bytes 3538952 | tf_op jit(solution)/shard_map/ppermute | solution.py:51
  119.3 37.7 %collective-permute-start.15 = (bf16[2,96,3840]{2,1,0:T(8,128)(2,1)S(1)}, bf16[2,96,3840]{2,1,0:T(8,128)(2,1)S(1)}, u32[]{:S(2)}, u32[]{:S(2)}) collective-permute-start(bf16[2,96,3840]{2,1,0:T(8,128)(2,1)S(1)} %pad_maximum_fusion.5), channel_id=1, source_target_pairs={{0,4},{1,5},{2,6},{3,7},{4,0},{5,1},{6,2},{7,3},{8,12},{9,13},{10,... | collective-permute-start | bytes 4423688 | tf_op jit(solution)/shard_map/ppermute | solution.py:51
  126.7 28.4 %collective-permute-start.14 = (bf16[2,96,3840]{2,1,0:T(8,128)(2,1)S(1)}, bf16[2,96,3840]{2,1,0:T(8,128)(2,1)S(1)}, u32[]{:S(2)}, u32[]{:S(2)}) collective-permute-start(bf16[2,96,3840]{2,1,0:T(8,128)(2,1)S(1)} %pad_maximum_fusion.5), channel_id=1, source_target_pairs={{0,16},{1,17},{2,18},{3,19},{4,12},{5,13},{6,14},{7,15},{8,24},{9,... | collective-permute-start | bytes 4423688 | tf_op jit(solution)/shard_map/ppermute | solution.py:51
  129.9 29.0 %collective-permute-start.9 = (bf16[2,96,2432]{2,1,0:T(8,128)(2,1)S(1)}, bf16[2,96,2432]{2,1,0:T(8,128)(2,1)S(1)}, u32[]{:S(2)}, u32[]{:S(2)}) collective-permute-start(bf16[2,96,2432]{2,1,0:T(8,128)(2,1)S(1)} %collective-permute-done.7), channel_id=1, source_target_pairs={{0,4},{1,5},{2,6},{3,7},{4,0},{5,1},{6,2},{7,3},{8,12},{9,13},{10,... | collective-permute-start | bytes 2801672 | tf_op jit(solution)/shard_map/ppermute | solution.py:51
  139.5 40.0 %collective-permute-start.23 = (bf16[2,384,768]{2,1,0:T(8,128)(2,1)}, bf16[2,384,768]{2,1,0:T(8,128)(2,1)}, u32[]{:S(2)}, u32[]{:S(2)}) collective-permute-start(bf16[2,384,768]{2,1,0:T(8,128)(2,1)} %collective-permute-done.21), channel_id=1, source_target_pairs={{0,4},{1,5},{2,6},{3,7},{4,0},{5,1},{6,2},{7,3},{8,12},{9,13},{10,... | collective-permute-start | bytes 3538952 | tf_op jit(solution)/shard_map/ppermute | solution.py:51
  155.2 28.3 %collective-permute-start.16 = (bf16[2,96,3840]{2,1,0:T(8,128)(2,1)S(1)}, bf16[2,96,3840]{2,1,0:T(8,128)(2,1)S(1)}, u32[]{:S(2)}, u32[]{:S(2)}) collective-permute-start(bf16[2,96,3840]{2,1,0:T(8,128)(2,1)S(1)} %collective-permute-done.14), channel_id=1, source_target_pairs={{0,4},{1,5},{2,6},{3,7},{4,0},{5,1},{6,2},{7,3},{8,12},{9,13},{10,... | collective-permute-start | bytes 4423688 | tf_op jit(solution)/shard_map/ppermute | solution.py:51
  261.3 15.2 %collective-permute-start.39 = (bf16[2,2,4,96,768]{4,3,2,1,0:T(8,128)(2,1)S(1)}, bf16[2,2,4,96,768]{4,3,2,1,0:T(8,128)(2,1)S(1)}, u32[]{:S(2)}, u32[]{:S(2)}) collective-permute-start(bf16[2,2,4,96,768]{4,3,2,1,0:T(8,128)(2,1)S(1)} %pad_maximum_fusion.2), channel_id=1, source_target_pairs={{0,4},{1,5},{2,6},{3,7},{4,0},{5,1},{6,2},{7,3},{8,12},{9,13},{10,... | collective-permute-start | bytes 7077896 | tf_op jit(solution)/shard_map/ppermute | solution.py:51
  262.9 23.3 %collective-permute-start.33 = (bf16[2,2,4,24,3840]{4,3,2,1,0:T(8,128)(2,1)S(1)}, bf16[2,2,4,24,3840]{4,3,2,1,0:T(8,128)(2,1)S(1)}, u32[]{:S(2)}, u32[]{:S(2)}) collective-permute-start(bf16[2,2,4,24,3840]{4,3,2,1,0:T(8,128)(2,1)S(1)} %pad_maximum_fusion.1), channel_id=1, source_target_pairs={{0,4},{1,5},{2,6},{3,7},{4,0},{5,1},{6,2},{7,3},{8,12},{9,13},{10,... | collective-permute-start | bytes 8847368 | tf_op jit(solution)/shard_map/ppermute | solution.py:51
  274.4 27.4 %collective-permute-start.24 = (bf16[320,768]{1,0:T(8,128)(2,1)S(1)}, bf16[320,768]{1,0:T(8,128)(2,1)S(1)}, u32[]{:S(2)}, u32[]{:S(2)}) collective-permute-start(bf16[320,768]{1,0:T(8,128)(2,1)S(1)} %get-tuple-element.78), channel_id=1, source_target_pairs={{0,3},{1,0},{2,1},{3,2},{4,7},{5,4},{6,5},{7,6},{8,11},{9,8},{10,9... | collective-permute-start | bytes 1474568 | tf_op jit(solution)/shard_map/ppermute | solution.py:51
  274.5 27.4 %collective-permute-start.26 = (bf16[320,768]{1,0:T(8,128)(2,1)S(1)}, bf16[320,768]{1,0:T(8,128)(2,1)S(1)}, u32[]{:S(2)}, u32[]{:S(2)}) collective-permute-start(bf16[320,768]{1,0:T(8,128)(2,1)S(1)} %get-tuple-element.79), channel_id=1, source_target_pairs={{0,1},{1,2},{2,3},{3,0},{4,5},{5,6},{6,7},{7,4},{8,9},{9,10},{10,1... | collective-permute-start | bytes 1474568 | tf_op jit(solution)/shard_map/ppermute | solution.py:51
  276.5 44.1 %collective-permute-start.25 = (bf16[320,768]{1,0:T(8,128)(2,1)S(1)}, bf16[320,768]{1,0:T(8,128)(2,1)S(1)}, u32[]{:S(2)}, u32[]{:S(2)}) collective-permute-start(bf16[320,768]{1,0:T(8,128)(2,1)S(1)} %get-tuple-element.80), channel_id=1, source_target_pairs={{0,2},{1,3},{2,0},{3,1},{4,6},{5,7},{6,4},{7,5},{8,10},{9,11},{10,... | collective-permute-start | bytes 1474568 | tf_op jit(solution)/shard_map/ppermute | solution.py:51
  283.6 45.9 %collective-permute-start.40 = (bf16[2,4,96,768]{3,2,1,0:T(8,128)(2,1)S(1)}, bf16[2,4,96,768]{3,2,1,0:T(8,128)(2,1)}, u32[]{:S(2)}, u32[]{:S(2)}) collective-permute-start(bf16[2,4,96,768]{3,2,1,0:T(8,128)(2,1)S(1)} %pad_maximum_fusion.8), channel_id=1, source_target_pairs={{0,16},{1,17},{2,18},{3,19},{4,12},{5,13},{6,14},{7,15},{8,24},{9,... | collective-permute-start | bytes 3538952 | tf_op jit(solution)/shard_map/ppermute | solution.py:51
  300.0 32.8 %collective-permute-start.34 = (bf16[2,4,24,3840]{3,2,1,0:T(8,128)(2,1)}, bf16[2,4,24,3840]{3,2,1,0:T(8,128)(2,1)}, u32[]{:S(2)}, u32[]{:S(2)}) collective-permute-start(bf16[2,4,24,3840]{3,2,1,0:T(8,128)(2,1)} %pad_maximum_fusion.6), channel_id=1, source_target_pairs={{0,16},{1,17},{2,18},{3,19},{4,12},{5,13},{6,14},{7,15},{8,24},{9,... | collective-permute-start | bytes 4423688 | tf_op jit(solution)/shard_map/ppermute | solution.py:51
  301.8 21.5 %collective-permute-start.30 = (bf16[24,2432]{1,0:T(8,128)(2,1)S(1)}, bf16[24,2432]{1,0:T(8,128)(2,1)S(1)}, u32[]{:S(2)}, u32[]{:S(2)}) collective-permute-start(bf16[24,2432]{1,0:T(8,128)(2,1)S(1)} %get-tuple-element.88), channel_id=1, source_target_pairs={{0,1},{1,2},{2,3},{3,0},{4,5},{5,6},{6,7},{7,4},{8,9},{9,10},{10,1... | collective-permute-start | bytes 350216 | tf_op jit(solution)/shard_map/ppermute | solution.py:51
  301.9 21.4 %collective-permute-start.32 = (bf16[24,2432]{1,0:T(8,128)(2,1)S(1)}, bf16[24,2432]{1,0:T(8,128)(2,1)S(1)}, u32[]{:S(2)}, u32[]{:S(2)}) collective-permute-start(bf16[24,2432]{1,0:T(8,128)(2,1)S(1)} %get-tuple-element.89), channel_id=1, source_target_pairs={{0,3},{1,0},{2,1},{3,2},{4,7},{5,4},{6,5},{7,6},{8,11},{9,8},{10,9... | collective-permute-start | bytes 350216 | tf_op jit(solution)/shard_map/ppermute | solution.py:51
  346.8 17.5 %collective-permute-start.43 = (bf16[96,768]{1,0:T(8,128)(2,1)S(1)}, bf16[96,768]{1,0:T(8,128)(2,1)S(1)}, u32[]{:S(2)}, u32[]{:S(2)}) collective-permute-start(bf16[96,768]{1,0:T(8,128)(2,1)S(1)} %get-tuple-element.86), channel_id=1, source_target_pairs={{0,2},{1,3},{2,0},{3,1},{4,6},{5,7},{6,4},{7,5},{8,10},{9,11},{10,... | collective-permute-start | bytes 442376 | tf_op jit(solution)/shard_map/ppermute | solution.py:51
  354.7 19.6 %collective-permute-start.37 = (bf16[24,3840]{1,0:T(8,128)(2,1)S(1)}, bf16[24,3840]{1,0:T(8,128)(2,1)S(1)}, u32[]{:S(2)}, u32[]{:S(2)}) collective-permute-start(bf16[24,3840]{1,0:T(8,128)(2,1)S(1)} %get-tuple-element.83), channel_id=1, source_target_pairs={{0,2},{1,3},{2,0},{3,1},{4,6},{5,7},{6,4},{7,5},{8,10},{9,11},{10,... | collective-permute-start | bytes 552968 | tf_op jit(solution)/shard_map/ppermute | solution.py:51
  (49 other events, 508.0 us)

commit v2 on v1

v2 whole, which is shorter than its diff:
```python
import functools
import itertools
import math

import jax
import jax.numpy as jnp
from jax import lax
from jax.experimental import pallas as pl
from jax.experimental.pallas import tpu as pltpu
from jax.sharding import PartitionSpec as P

HEAD_DIM = 64
PAIR = 2 * HEAD_DIM
EPSILON = 1e-12
AXES = ("page", "band")
SLAB = 256
BF16, F32 = jnp.bfloat16, jnp.float32
VMEM_LIMIT = 56 * 2**20
CHEAP = pl.CostEstimate(flops=1024, bytes_accessed=1024, transcendentals=0)


def dot(left, right):
    return lax.dot_general(left, right, (((1,), (0,)), ((), ())), preferred_element_type=F32)


def times_transposed(left, right):
    return lax.dot_general(left, right, (((1,), (1,)), ((), ())), preferred_element_type=F32)


def outer_sum(left, right):
    return lax.dot_general(left, right, (((0,), (0,)), ((), ())), preferred_element_type=F32)


class Grid:
    def __init__(self, pages, bands):
        self.side = math.isqrt(pages // 2)
        assert self.side * self.side * 2 == pages
        self.bands = bands
        self.devices = pages * bands
        self.quads = self.side * self.side

    def linear(self, i, j, c, z):
        return ((i * self.side + j) * 2 + c) * self.bands + z

    def permute(self, array, move):
        side, bands = self.side, self.bands
        pairs = []
        for i, j, c, z in itertools.product(range(side), range(side), range(2), range(bands)):
            ti, tj, tc, tz = move(i, j, c, z)
            pairs.append((self.linear(i, j, c, z), self.linear(ti % side, tj % side, tc, tz % bands)))
        return lax.ppermute(array, AXES, pairs)

    def along_z(self, array, step):
        return self.permute(array, lambda i, j, c, z: (i, j, c, z + step))

    def near(self, array, step):
        return self.permute(
            array, lambda i, j, c, z: (i, j + step, c, z) if c == 0 else (i + step, j, c, z)
        )

    def far(self, array, step):
        return self.permute(
            array, lambda i, j, c, z: (i + step, j, c, z) if c == 0 else (i, j + step, c, z)
        )

    def across(self, array):
        return self.permute(array, lambda i, j, c, z: (i, j, 1 - c, z))

    def place(self):
        page, z = lax.axis_index("page"), lax.axis_index("band")
        return page // (2 * self.side), (page // 2) % self.side, page % 2, z


def after(value, *others):
    return lax.optimization_barrier((value, others))[0]


def z_direct(grid, shard):
    return [shard] + [grid.along_z(shard, step) for step in range(1, grid.bands)]


def z_ring(grid, shard):
    pieces = [shard]
    for _ in range(1, grid.bands):
        pieces.append(grid.along_z(pieces[-1], 1))
    return pieces


class Gather:
    def __init__(self, grid, pieces):
        self.grid = grid
        rows, width = pieces[0].shape
        z = lax.axis_index("band")
        block = jnp.zeros((grid.bands, rows, width), pieces[0].dtype)
        for step, piece in enumerate(pieces):
            block = lax.dynamic_update_slice(block, piece[None], ((z - step) % grid.bands, 0, 0))
        self.block = block.reshape(grid.bands * rows, width)

    def near_step(self, *pins):
        block = after(self.block, *pins)
        got = [self.grid.near(block, step) for step in range(1, self.grid.side)]
        self.near_all = jnp.stack([self.block] + got)

    def far_step(self, *pins):
        near_all = after(self.near_all, *pins)
        self.far_all = [self.grid.far(near_all, step) for step in range(1, self.grid.side)]

    def core_step(self, *pins):
        parts = [self.near_all] + self.far_all
        first = self.grid.across(after(self.near_all, *pins))
        return parts + [first] + [self.grid.across(item) for item in self.far_all]


def part_copies(grid, parts, whole, sems):
    i, j, c, _ = grid.place()
    tall = parts[0].shape[1]
    copies = []
    for d in range(2):
        core = (c + d) % 2
        for a in range(grid.side):
            for b in range(grid.side):
                di = jnp.where(core == 0, a, b)
                dj = jnp.where(core == 0, b, a)
                up = (i - di + grid.side) % grid.side
                left = (j - dj + grid.side) % grid.side
                index = (up * grid.side + left) * 2 + core
                copies.append(
                    pltpu.make_async_copy(
                        parts[d * grid.side + a].at[b],
                        whole.at[pl.ds(pl.multiple_of(index * tall, 8), tall), :],
                        sems.at[len(copies)],
                    )
                )
    return copies


def store_blocks(grid, source, first, cols, keep, send):
    i, j, c, _ = grid.place()
    tall = keep.shape[1]
    for n in range(source.shape[0] // tall):
        block = first + n
        core = block % 2
        ti, tj = block // (2 * grid.side), (block // 2) % grid.side
        di = (ti - i + grid.side) % grid.side
        dj = (tj - j + grid.side) % grid.side
        slot = di * grid.side + dj if core == 0 else dj * grid.side + di
        rows = slice(n * tall, (n + 1) * tall)

        @pl.when(c == core)
        def _():
            keep[slot, :, cols] = source[rows, :].astype(BF16)

        @pl.when(c != core)
        def _():
            send[slot, :, cols] = source[rows, :].astype(BF16)


class Sum:
    def __init__(self, grid, keep, send):
        self.grid, self.send = grid, send
        self.terms = [keep]

    def total(self, at):
        result = self.terms[0][at].astype(F32)
        for item in self.terms[1:]:
            result = result + item[at].astype(F32)
        return result

    def core_step(self, *pins):
        side = self.grid.side
        got = self.grid.across(self.send)
        self.terms = after(self.terms, *pins) + [got]
        self.send = [self.total(slice(a * side, (a + 1) * side)).astype(BF16) for a in range(1, side)]

    def far_step(self, *pins):
        side = self.grid.side
        got = [self.grid.far(item, a) for a, item in enumerate(self.send, 1)]
        self.terms = after(self.terms, *pins) + got
        self.send = [self.total(b).astype(BF16) for b in range(1, side)]

    def near_step(self, *pins):
        grid = self.grid
        got = [grid.near(item, b)[None] for b, item in enumerate(self.send, 1)]
        self.terms = after(self.terms, *pins) + got
        own = self.total(0)
        own = own.reshape(grid.bands, own.shape[0] // grid.bands, own.shape[1])
        z = lax.axis_index("band")
        self.own = lax.dynamic_index_in_dim(own, z, 0, False)
        self.send = [
            lax.dynamic_index_in_dim(own, (z + step) % grid.bands, 0, False).astype(BF16)
            for step in range(1, grid.bands)
        ]

    def z_step(self):
        for step, item in enumerate(self.send, 1):
            self.own = self.own + self.grid.along_z(item, step).astype(F32)
        return self.own


def pack_kernel(lengths, permutation, *refs):
    vectors, bias = refs[:8], refs[8]
    wq, wk, wv, wo, wi, wc = refs[9:15]
    a_out, b_out, c_out, doc_out = refs[15:19]
    stage, tall = refs[19:]
    rows, width = wq.shape
    docs = lengths.shape[1]
    tokens = permutation.shape[1]
    earlier = lax.broadcasted_iota(jnp.int32, (docs, docs), 1) <= lax.broadcasted_iota(
        jnp.int32, (docs, docs), 0
    )
    ends = jnp.sum(jnp.where(earlier, lengths[...], 0).astype(F32), axis=1, keepdims=True)
    marks = jnp.sum(
        jnp.where(permutation[...].astype(F32) >= ends, 1.0, 0.0), axis=0, keepdims=True
    )
    doc_out[...] = marks
    for n, item in enumerate((wq, None, None)):
        if item is not None:
            a_out[:, n * width : (n + 1) * width] = item[...].astype(BF16)
    for pair in range(width // PAIR):
        at = width + 2 * pair * PAIR
        cols = slice(pair * PAIR, (pair + 1) * PAIR)
        a_out[:, at : at + PAIR] = wk[:, cols].astype(BF16)
        a_out[:, at + PAIR : at + 2 * PAIR] = wv[:, cols].astype(BF16)
    stage[...] = jnp.zeros_like(stage)
    for n, item in enumerate(vectors):
        stage[n : n + 1, 0:rows] = item[...].reshape(1, rows)
    tall[...] = jnp.transpose(stage[...])
    tall[0:1, 16 : 16 + bias.shape[0]] = bias[...].reshape(1, bias.shape[0])
    a_out[:, 3 * width : 3 * width + 128] = tall[0:rows, :].astype(BF16)
    tall[...] = jnp.zeros_like(tall)
    for n in range(3):
        count = min(128, tokens - n * 128)
        tall[n : n + 1, 0:count] = marks[:, n * 128 : n * 128 + count]
    a_out[:, 3 * width + 128 :] = tall[0:rows, :].astype(BF16)
    b_out[:, :width] = wo[...].astype(BF16)
    b_out[:, width:] = wi[...].astype(BF16)
    c_out[...] = wc[...].astype(BF16)


def pack(lengths, permutation, vectors, bias, weights):
    rows, width = weights[0].shape
    wide = weights[4].shape[1]
    tokens = permutation.shape[1]
    assert tokens <= 3 * 128 and bias.shape[0] <= 112 and rows <= 128
    vmem = pl.BlockSpec(memory_space=pltpu.VMEM)
    return pl.pallas_call(
        pack_kernel,
        in_specs=[vmem] * 17,
        out_specs=[vmem] * 4,
        out_shape=[
            jax.ShapeDtypeStruct((rows, 3 * width + SLAB), BF16),
            jax.ShapeDtypeStruct((rows, width + wide), BF16),
            jax.ShapeDtypeStruct(weights[5].shape, BF16),
            jax.ShapeDtypeStruct((1, tokens), F32),
        ],
        scratch_shapes=[pltpu.VMEM((128, 128), F32), pltpu.VMEM((128, 128), F32)],
        compiler_params=pltpu.CompilerParams(vmem_limit_bytes=VMEM_LIMIT),
        cost_estimate=CHEAP,
        name="pack",
    )(lengths, permutation, *vectors, bias, *weights)


def head_mask(rows, head):
    lanes = lax.broadcasted_iota(jnp.int32, (rows, PAIR), 1)
    return (lanes // HEAD_DIM) == head


def attend_kernel(grid, pieces, parts, *refs):
    hidden, refs = refs[:pieces], refs[pieces:]
    part_refs, refs = refs[:parts], refs[parts:]
    own_doc, all_doc = refs[:2]
    q_out, kv_out, att_out, log_out, vec_out, bias_out, bias, weights, slab, sems = refs[2:]
    tokens = q_out.shape[0]
    keys = kv_out.shape[0]
    width = weights.shape[0]
    step = q_out.shape[1]
    group = pl.program_id(0)

    @pl.when(group == 0)
    def _():
        copies = part_copies(grid, part_refs, weights, sems)
        for copy in copies:
            copy.start()
        bias[...] = jnp.where(own_doc[...] == all_doc[...], 0.0, -1e30).astype(F32)
        for copy in copies:
            copy.wait()
        slab[...] = weights[:, 3 * width : 3 * width + 128].astype(F32)
        vec_out[...] = jnp.transpose(slab[...])[0:16, :]
        rows = width // grid.devices
        count = bias_out.shape[1] // grid.devices
        for n in range(grid.devices):
            bias_out[:, n * count : (n + 1) * count] = slab[n * rows : n * rows + 1, 16 : 16 + count]

    at = pl.multiple_of(group * step, step)
    query_bias = vec_out[0:1, pl.ds(at, step)]
    value_bias = vec_out[1:2, pl.ds(at, step)]
    q_out[...] = (dot(hidden[0][...], weights[:, pl.ds(at, step)]) + query_bias).astype(BF16)
    pairs = step // PAIR
    for p in range(pieces):
        rows = slice(p * tokens, (p + 1) * tokens)
        for pair in range(pairs):
            there = pl.multiple_of(width + 2 * at + 2 * pair * PAIR, 2 * PAIR)
            both = dot(hidden[p][...], weights[:, pl.ds(there, 2 * PAIR)])
            to = 2 * pair * PAIR
            kv_out[rows, to : to + PAIR] = both[:, :PAIR].astype(BF16)
            value = both[:, PAIR:] + value_bias[:, pair * PAIR : (pair + 1) * PAIR]
            kv_out[rows, to + PAIR : to + 2 * PAIR] = value.astype(BF16)
    lane = lax.broadcasted_iota(jnp.int32, (tokens, 128), 1)
    logs = jnp.zeros((tokens, 128), F32)
    ones = jnp.ones((keys, PAIR), BF16)
    for pair in range(pairs):
        cols = slice(pair * PAIR, (pair + 1) * PAIR)
        query = q_out[:, cols]
        key = kv_out[:, 2 * pair * PAIR : (2 * pair + 1) * PAIR]
        value = jnp.concatenate([kv_out[:, (2 * pair + 1) * PAIR : (2 * pair + 2) * PAIR], ones], axis=1)
        outs = []
        for head in range(2):
            picked = jnp.where(head_mask(tokens, head), query * HEAD_DIM**-0.5, 0).astype(BF16)
            scores = times_transposed(picked, key) + bias[...]
            peak = jnp.max(scores, axis=1, keepdims=True)
            weights = jnp.exp(scores - peak).astype(BF16)
            both = dot(weights, value)
            outs.append(both[:, :PAIR] / both[:, PAIR:])
            total = peak + jnp.log(both[:, PAIR:])
            logs = jnp.where(lane == pair * 2 + head, total, logs)
        att_out[:, cols] = jnp.where(head_mask(tokens, 0), outs[0], outs[1]).astype(BF16)
    log_out[...] = logs[None]


ANY = pl.BlockSpec(memory_space=pl.ANY)
VMEM = pl.BlockSpec(memory_space=pltpu.VMEM)


def attend(grid, hidden, parts, own_doc, all_doc, wide):
    pieces = len(hidden)
    tokens, width = hidden[0].shape
    keys = pieces * tokens
    step = 256
    groups = width // step
    whole = lambda shape: pl.BlockSpec(shape, lambda g: (0, 0))
    tall = lambda rows: pl.BlockSpec((rows, step), lambda g: (0, g))
    return pl.pallas_call(
        functools.partial(attend_kernel, grid, pieces, len(parts)),
        grid=(groups,),
        in_specs=[whole(item.shape) for item in hidden]
        + [ANY] * len(parts)
        + [whole(own_doc.shape), whole(all_doc.shape)],
        out_specs=[
            tall(tokens),
            pl.BlockSpec((keys, 2 * step), lambda g: (0, g)),
            tall(tokens),
            pl.BlockSpec((1, tokens, 128), lambda g: (g, 0, 0)),
            whole((16, width)),
            whole((1, wide)),
        ],
        out_shape=[
            jax.ShapeDtypeStruct((tokens, width), BF16),
            jax.ShapeDtypeStruct((keys, 2 * width), BF16),
            jax.ShapeDtypeStruct((tokens, width), BF16),
            jax.ShapeDtypeStruct((groups, tokens, 128), F32),
            jax.ShapeDtypeStruct((16, width), F32),
            jax.ShapeDtypeStruct((1, wide), F32),
        ],
        scratch_shapes=[
            pltpu.VMEM((tokens, keys), F32),
            pltpu.VMEM((width, parts[0].shape[2]), BF16),
            pltpu.VMEM((width, 128), F32),
            pltpu.SemaphoreType.DMA((2 * grid.quads,)),
        ],
        compiler_params=pltpu.CompilerParams(vmem_limit_bytes=VMEM_LIMIT),
        cost_estimate=CHEAP,
        name="attend",
    )(*hidden, *parts, own_doc, all_doc)


def attend_back_kernel(start, q, kv, grad, att, logs, own_doc, doc, dq_out, dkv_out, sum_out, bias):
    tokens = q.shape[0]
    pair = pl.program_id(0) + start

    @pl.when(pair == start)
    def _():
        bias[...] = jnp.where(own_doc[...] == doc[...], 0.0, -1e30).astype(F32)

    lane = lax.broadcasted_iota(jnp.int32, (tokens, 128), 1)
    key, value = kv[:, :PAIR], kv[:, PAIR:]
    product = grad[...].astype(F32) * att[...].astype(F32)
    dq, dk, dv = [], 0.0, 0.0
    for head in range(2):
        mask = head_mask(tokens, head)
        query = jnp.where(mask, q[...] * HEAD_DIM**-0.5, 0).astype(BF16)
        part = jnp.where(mask, grad[...], 0).astype(BF16)
        slot = (pair % 2) * 2 + head
        log_total = jnp.sum(jnp.where(lane == slot, logs[0], 0.0), axis=1, keepdims=True)
        inner = jnp.sum(jnp.where(mask, product, 0.0), axis=1, keepdims=True)
        weights = jnp.exp(times_transposed(query, key) + bias[...] - log_total)
        back = (weights * (times_transposed(part, value) - inner)).astype(BF16)
        dq.append(dot(back, key) * HEAD_DIM**-0.5)
        dk = dk + outer_sum(back, query)
        dv = dv + outer_sum(weights.astype(BF16), part)
    dq_low = jnp.where(head_mask(tokens, 0), dq[0], dq[1]).astype(BF16)
    dq_out[...] = dq_low
    dkv_out[:, :PAIR] = dk.astype(BF16)
    dv_low = dv.astype(BF16)
    dkv_out[:, PAIR:] = dv_low
    sum_out[0:1, :] = column_sum(dq_low)
    sum_out[1:2, :] = column_sum(dv_low)


def attend_back(start, pairs, q, kv, grad, att, logs, own_doc, all_doc):
    tokens = q.shape[0]
    keys = kv.shape[0]
    short = pl.BlockSpec((tokens, PAIR), lambda g: (0, start + g))
    whole = lambda shape: pl.BlockSpec(shape, lambda g: (0, 0))
    return pl.pallas_call(
        functools.partial(attend_back_kernel, start),
        grid=(pairs,),
        in_specs=[
            short,
            pl.BlockSpec((keys, 2 * PAIR), lambda g: (0, start + g)),
            short,
            short,
            pl.BlockSpec((1, tokens, 128), lambda g: ((start + g) // 2, 0, 0)),
            whole(own_doc.shape),
            whole(all_doc.shape),
        ],
        out_specs=[
            pl.BlockSpec((tokens, PAIR), lambda g: (0, g)),
            pl.BlockSpec((keys, 2 * PAIR), lambda g: (0, g)),
            pl.BlockSpec((8, PAIR), lambda g: (0, g)),
        ],
        out_shape=[
            jax.ShapeDtypeStruct((tokens, pairs * PAIR), BF16),
            jax.ShapeDtypeStruct((keys, 2 * pairs * PAIR), BF16),
            jax.ShapeDtypeStruct((8, pairs * PAIR), F32),
        ],
        scratch_shapes=[pltpu.VMEM((tokens, keys), F32)],
        compiler_params=pltpu.CompilerParams(vmem_limit_bytes=VMEM_LIMIT),
        cost_estimate=CHEAP,
        name="attend_back",
    )(q, kv, grad, att, logs, own_doc, all_doc)


def interleave(key, value):
    rows, width = key.shape
    split = lambda item: item.reshape(rows, width // PAIR, 1, PAIR)
    return jnp.concatenate([split(key), split(value)], axis=2).reshape(rows, 2 * width)


def part_of(both, which):
    rows, width = both.shape
    return both.reshape(rows, width // (2 * PAIR), 2, PAIR)[:, :, which].reshape(rows, width // 2)


def row_mean(values):
    return jnp.mean(values, axis=-1, keepdims=True)


def column_sum(values):
    return jnp.sum(values.astype(F32), axis=0, keepdims=True)


def norm_back(grad_out, normed, inverse, scale_gain):
    grad_normed = grad_out * scale_gain
    inner = grad_normed - row_mean(grad_normed) - normed * row_mean(grad_normed * normed)
    return inner * inverse


def normalize(values):
    centred = values - row_mean(values)
    inverse = lax.rsqrt(row_mean(centred * centred) + EPSILON)
    return centred * inverse, inverse


def middle_kernel(grid, parts, att, hidden, cotangent, vec, b_expand, *refs):
    parts_b, parts_c, refs = refs[:parts], refs[parts : 2 * parts], refs[2 * parts :]
    result, first_out, normed_out, inverse_out, slope, second_out, low_out, keep, send, sums = refs[:10]
    wb, wc, active, total, sem_b, sem_c = refs[10:]
    width, wide = wb.shape[0], wc.shape[0]
    copies_b = part_copies(grid, parts_b, wb, sem_b)
    copies_c = part_copies(grid, parts_c, wc, sem_c)
    for copy in copies_b + copies_c:
        copy.start()
    for copy in copies_b:
        copy.wait()
    mixed = dot(att[...], wb[:, :width]) + vec[2:3, :]
    normed, inverse = normalize(hidden[...].astype(F32) + mixed)
    normed_out[...] = normed
    inverse_out[...] = jnp.broadcast_to(inverse, inverse_out.shape)
    first = normed * vec[3:4, :] + vec[4:5, :]
    first_out[...] = first.astype(BF16)
    for n in range(wide // width):
        cols = slice(n * width, (n + 1) * width)
        into = dot(first_out[...], wb[:, width + n * width : width + (n + 1) * width]) + b_expand[:, cols]
        chance = 0.5 * (1.0 + lax.erf(into * (0.5**0.5)))
        density = jnp.exp(-0.5 * into * into) * ((2.0 * math.pi) ** -0.5)
        active[:, cols] = (into * chance).astype(BF16)
        slope[:, cols] = (chance + into * density).astype(BF16)
    for copy in copies_c:
        copy.wait()
    contracted = dot(active[...], wc[...]) + vec[5:6, :]
    normed, inverse = normalize(first + contracted)
    result[...] = (normed * vec[6:7, :] + vec[7:8, :]).astype(BF16)
    grad = cotangent[...].astype(F32)
    second = norm_back(grad, normed, inverse, vec[6:7, :])
    second_out[...] = second
    low = second.astype(BF16)
    low_out[...] = low
    sums[...] = jnp.zeros_like(sums)
    sums[5:6, :] = column_sum(low)
    sums[6:7, :] = column_sum(grad * normed)
    sums[7:8, :] = column_sum(grad)
    blocks = width // keep.shape[1]
    for n in range(wide // width):
        total[...] = outer_sum(active[:, n * width : (n + 1) * width], low)
        store_blocks(grid, total, n * blocks, slice(0, width), keep, send)


def middle(grid, att, hidden, cotangent, vec, b_expand, parts_b, parts_c):
    tokens, width = hidden.shape
    wide = b_expand.shape[1]
    blocks = jax.ShapeDtypeStruct((grid.quads,) + parts_c[0].shape[1:], BF16)
    return pl.pallas_call(
        functools.partial(middle_kernel, grid, len(parts_b)),
        in_specs=[VMEM] * 5 + [ANY] * (2 * len(parts_b)),
        out_specs=[VMEM] * 10,
        out_shape=[
            jax.ShapeDtypeStruct((tokens, width), BF16),
            jax.ShapeDtypeStruct((tokens, width), BF16),
            jax.ShapeDtypeStruct((tokens, width), F32),
            jax.ShapeDtypeStruct((tokens, 128), F32),
            jax.ShapeDtypeStruct((tokens, wide), BF16),
            jax.ShapeDtypeStruct((tokens, width), F32),
            jax.ShapeDtypeStruct((tokens, width), BF16),
            blocks,
            blocks,
            jax.ShapeDtypeStruct((8, width), F32),
        ],
        scratch_shapes=[
            pltpu.VMEM((width, width + wide), BF16),
            pltpu.VMEM((wide, width), BF16),
            pltpu.VMEM((tokens, wide), BF16),
            pltpu.VMEM((width, width), F32),
            pltpu.SemaphoreType.DMA((2 * grid.quads,)),
            pltpu.SemaphoreType.DMA((2 * grid.quads,)),
        ],
        compiler_params=pltpu.CompilerParams(vmem_limit_bytes=VMEM_LIMIT),
        cost_estimate=CHEAP,
        name="middle",
    )(att, hidden, cotangent, vec, b_expand, *parts_b, *parts_c)


def dense_back_kernel(grid, parts, att, first, normed, inverse, slope, second, low, vec, *refs):
    parts_b, parts_c, refs = refs[:parts], refs[parts : 2 * parts], refs[2 * parts :]
    grad_sum, att_back, keep, send, sums, bias_sum = refs[:6]
    wb, wc, back, total, sem_b, sem_c = refs[6:]
    width, wide = wb.shape[0], wc.shape[0]
    copies_b = part_copies(grid, parts_b, wb, sem_b)
    copies_c = part_copies(grid, parts_c, wc, sem_c)
    for copy in copies_c + copies_b:
        copy.start()
    for copy in copies_c:
        copy.wait()
    for n in range(wide // width):
        cols = slice(n * width, (n + 1) * width)
        piece = (times_transposed(low[...], wc[cols, :]) * slope[:, cols].astype(F32)).astype(BF16)
        back[:, cols] = piece
        bias_sum[:, cols] = column_sum(piece)
    for copy in copies_b:
        copy.wait()
    grad_first = second[...] + times_transposed(back[...], wb[:, width:])
    grad = norm_back(grad_first, normed[...], inverse[:, 0:1], vec[3:4, :])
    grad_sum[...] = grad
    mixed = grad.astype(BF16)
    att_back[...] = times_transposed(mixed, wb[:, :width]).astype(BF16)
    sums[...] = jnp.zeros_like(sums)
    sums[2:3, :] = column_sum(mixed)
    sums[3:4, :] = column_sum(grad_first * normed[...])
    sums[4:5, :] = column_sum(grad_first)
    total[...] = outer_sum(att[...], mixed)
    store_blocks(grid, total, 0, slice(0, width), keep, send)
    for n in range(wide // width):
        total[...] = outer_sum(first[...], back[:, n * width : (n + 1) * width])
        store_blocks(grid, total, 0, slice((n + 1) * width, (n + 2) * width), keep, send)


def dense_back(grid, att, first, normed, inverse, slope, second, low, vec, parts_b, parts_c):
    tokens, width = att.shape
    wide = slope.shape[1]
    blocks = jax.ShapeDtypeStruct((grid.quads,) + parts_b[0].shape[1:], BF16)
    return pl.pallas_call(
        functools.partial(dense_back_kernel, grid, len(parts_b)),
        in_specs=[VMEM] * 8 + [ANY] * (2 * len(parts_b)),
        out_specs=[VMEM] * 6,
        out_shape=[
            jax.ShapeDtypeStruct((tokens, width), F32),
            jax.ShapeDtypeStruct((tokens, width), BF16),
            blocks,
            blocks,
            jax.ShapeDtypeStruct((8, width), F32),
            jax.ShapeDtypeStruct((1, wide), F32),
        ],
        scratch_shapes=[
            pltpu.VMEM((width, width + wide), BF16),
            pltpu.VMEM((wide, width), BF16),
            pltpu.VMEM((tokens, wide), BF16),
            pltpu.VMEM((width, width), F32),
            pltpu.SemaphoreType.DMA((2 * grid.quads,)),
            pltpu.SemaphoreType.DMA((2 * grid.quads,)),
        ],
        compiler_params=pltpu.CompilerParams(vmem_limit_bytes=VMEM_LIMIT),
        cost_estimate=CHEAP,
        name="dense_back",
    )(att, first, normed, inverse, slope, second, low, vec, *parts_b, *parts_c)


def input_back_kernel(grid, parts, grad_sum, dq0, dq1, dkv0, dkv1, *refs):
    part_refs, outs = refs[:parts], refs[parts:-2]
    weights, sems = refs[-2:]
    tokens = grad_sum.shape[0]
    width = weights.shape[0]
    half = dkv0.shape[1]
    copies = part_copies(grid, part_refs, weights, sems)
    for copy in copies:
        copy.start()
    for copy in copies:
        copy.wait()
    for piece in range(len(outs) - 1, -1, -1):
        rows = slice(piece * tokens, (piece + 1) * tokens)
        back = times_transposed(dkv0[rows, :], weights[:, width : width + half])
        back = back + times_transposed(dkv1[rows, :], weights[:, width + half : 3 * width])
        if piece == 0:
            back = back + times_transposed(dq0[...], weights[:, : half // 2])
            back = back + times_transposed(dq1[...], weights[:, half // 2 : width])
            back = back + grad_sum[...]
        outs[piece][...] = back.astype(outs[piece].dtype)


def input_back(grid, grad_sum, first_part, last_part, parts):
    tokens, width = grad_sum.shape
    return pl.pallas_call(
        functools.partial(input_back_kernel, grid, len(parts)),
        in_specs=[VMEM] * 5 + [ANY] * len(parts),
        out_specs=[VMEM] * grid.bands,
        out_shape=[jax.ShapeDtypeStruct((tokens, width), F32)]
        + [jax.ShapeDtypeStruct((tokens, width), BF16)] * (grid.bands - 1),
        scratch_shapes=[
            pltpu.VMEM((width, parts[0].shape[2]), BF16),
            pltpu.SemaphoreType.DMA((2 * grid.quads,)),
        ],
        compiler_params=pltpu.CompilerParams(vmem_limit_bytes=VMEM_LIMIT),
        cost_estimate=CHEAP,
        name="input_back",
    )(grad_sum, first_part[0], last_part[0], first_part[1], last_part[1], *parts)


def weight_back_kernel(grid, pieces, *refs):
    hidden, refs = refs[:pieces], refs[pieces:]
    dq0, dq1, dkv0, dkv1, sum0, sum1, sum2, sum3, bias_sum, keep, send, every, total, stage, slab = refs
    tokens, width = hidden[0].shape
    half = dkv0.shape[1]
    for n in range(pieces):
        every[n * tokens : (n + 1) * tokens, :] = hidden[n][...]
    for n, item in enumerate((dkv0, dkv1)):
        total[:, 0:half] = outer_sum(every[...], item[...])
        store_blocks(grid, total, 0, slice(width + n * half, width + (n + 1) * half), keep, send)
    for n, item in enumerate((dq0, dq1)):
        total[:, n * half // 2 : (n + 1) * half // 2] = outer_sum(hidden[0][...], item[...])
    store_blocks(grid, total, 0, slice(0, width), keep, send)
    stage[...] = jnp.zeros_like(stage)
    stage[0:8, :] = sum2[...] + sum3[...]
    for n, item in enumerate((sum0, sum1)):
        stage[0:2, n * half // 2 : (n + 1) * half // 2] = item[0:2, :]
    slab[:, :128] = jnp.transpose(stage[...])
    slab[:, 128:] = jnp.zeros((width, SLAB - 128), F32)
    rows = width // grid.devices
    count = bias_sum.shape[1] // grid.devices
    for n in range(grid.devices):
        slab[n * rows : n * rows + 1, 16 : 16 + count] = bias_sum[:, n * count : (n + 1) * count]
    store_blocks(grid, slab, 0, slice(3 * width, 3 * width + SLAB), keep, send)


def weight_back(grid, hidden, first_part, last_part, sums, bias_sum):
    pieces = len(hidden)
    tokens, width = hidden[0].shape
    tall = width // (2 * grid.quads)
    blocks = jax.ShapeDtypeStruct((grid.quads, tall, 3 * width + SLAB), BF16)
    return pl.pallas_call(
        functools.partial(weight_back_kernel, grid, pieces),
        in_specs=[VMEM] * (pieces + 9),
        out_specs=[VMEM] * 2,
        out_shape=[blocks, blocks],
        scratch_shapes=[
            pltpu.VMEM((pieces * tokens, width), BF16),
            pltpu.VMEM((width, width), F32),
            pltpu.VMEM((128, width), F32),
            pltpu.VMEM((width, SLAB), F32),
        ],
        compiler_params=pltpu.CompilerParams(vmem_limit_bytes=VMEM_LIMIT),
        cost_estimate=CHEAP,
        name="weight_back",
    )(
        *hidden,
        first_part[0],
        last_part[0],
        first_part[1],
        last_part[1],
        first_part[2],
        last_part[2],
        *sums,
        bias_sum,
    )


def per_device(
    grid,
    hidden_in,
    lengths,
    permutation,
    query_weight,
    query_bias,
    key_weight,
    value_weight,
    value_bias,
    mix_weight,
    mix_bias,
    first_gain,
    first_shift,
    expand_weight,
    expand_bias,
    contract_weight,
    contract_bias,
    second_gain,
    second_shift,
    cotangent,
):
    tokens, width = hidden_in.shape
    wide = contract_weight.shape[0] * grid.devices
    rows = query_weight.shape[0]
    bands = grid.bands

    vectors = [query_bias, value_bias, mix_bias, first_gain, first_shift, contract_bias, second_gain, second_shift]
    weights = [query_weight, key_weight, value_weight, mix_weight, expand_weight, contract_weight]
    shard_a, shard_b, shard_c, doc = pack(lengths, permutation, vectors, expand_bias, weights)

    messages = [hidden_in, grid.along_z(hidden_in, 1)]
    pieces_a = z_direct(grid, shard_a)
    pieces_b = z_direct(grid, after(shard_b, *pieces_a))
    gather_a = Gather(grid, pieces_a)
    gather_a.near_step()
    messages.append(grid.along_z(after(messages[-1], *pieces_a), 1))
    pieces_c = z_direct(grid, after(shard_c, *pieces_b, gather_a.near_all))
    gather_b, gather_c = Gather(grid, pieces_b), Gather(grid, pieces_c)
    gather_a.far_step()
    gather_b.near_step()
    for step in range(3, bands):
        messages.append(grid.along_z(after(messages[-1], *pieces_b), 1))
    gather_c.near_step(*gather_a.far_all)
    gather_b.far_step(*gather_a.far_all)
    parts_a = gather_a.core_step()
    gather_c.far_step()
    messages[0] = after(messages[0], gather_c.near_all, gather_b.near_all)
    parts_b = gather_b.core_step()

    docs_of = [doc] + [
        item[0:3, 3 * width + 128 :].astype(F32).reshape(1, 3 * 128)[:, :tokens] for item in pieces_a[1:]
    ]
    all_doc = jnp.concatenate(docs_of, axis=1)
    own_doc = doc.reshape(tokens, 1)
    q, kv, attended, logs, vec, b_expand = attend(grid, messages, parts_a, own_doc, all_doc, wide)
    gather_c.far_all = after(gather_c.far_all, attended)
    parts_c = gather_c.core_step()
    result, first, normed, inverse, slope, second, low, keep, send, sums_two = middle(
        grid, attended, hidden_in, cotangent, vec, b_expand, parts_b, parts_c
    )
    sum_c = Sum(grid, keep, send)
    sum_c.core_step()
    low = after(low, *sum_c.send)
    grad_sum, attended_back, keep, send, sums_one, d_b_expand = dense_back(
        grid, attended, first, normed, inverse, slope, second, low, vec, parts_b, parts_c
    )
    sum_b = Sum(grid, keep, send)
    sum_c.far_step(grad_sum)
    attended_back = after(attended_back, sum_c.send)

    pairs = width // PAIR
    half = pairs // 2
    first_part = attend_back(0, half, q, kv, attended_back, attended, logs, own_doc, all_doc)
    sum_c.near_step(first_part)
    sum_b.core_step(sum_c.send)
    attended_back = after(attended_back, sum_b.send, sum_c.send)
    last_part = attend_back(half, pairs - half, q, kv, attended_back, attended, logs, own_doc, all_doc)
    backs = input_back(grid, grad_sum, first_part, last_part, parts_a)
    sum_b.far_step(backs)
    last_part = after(last_part, backs, sum_b.send)
    keep, send = weight_back(grid, messages, first_part, last_part, (sums_two, sums_one), d_b_expand)
    sum_a = Sum(grid, keep, send)
    sent = backs[bands - 1]
    for piece in range(bands - 1, 0, -1):
        got = grid.along_z(sent, -1)
        pins = (keep,) if piece == bands - 1 else tuple(sum_b.send)
        sent = after(backs[piece - 1], *pins).astype(F32) + got.astype(F32)
        if piece > 1:
            sent = sent.astype(BF16)
        if piece == bands - 1:
            sum_a.core_step(sent)
            sum_b.near_step(sum_a.send)
        elif piece == bands - 2:
            sum_a.far_step(sent)
    grad_input = sent
    sum_a.near_step()
    d_contract = sum_c.z_step()
    d_b = sum_b.z_step()
    d_a = sum_a.z_step()
    slab = d_a[:, 3 * width :]
    small = [slab[:, n] for n in range(8)]
    d_both = d_a[:, width : 3 * width]
    return (
        result,
        grad_input.astype(BF16),
        d_a[:, :width],
        small[0],
        part_of(d_both, 0),
        part_of(d_both, 1),
        small[1],
        d_b[:, :width],
        small[2],
        small[3],
        small[4],
        d_b[:, width:],
        slab[0, 16 : 16 + expand_bias.shape[0]],
        d_contract,
        small[5],
        small[6],
        small[7],
    )


def solution(mesh):
    grid = Grid(mesh.shape["page"], mesh.shape["band"])
    matrix, vector = P(AXES, None), P(AXES)
    parameters = (
        matrix,
        vector,
        matrix,
        matrix,
        vector,
        matrix,
        vector,
        vector,
        vector,
        matrix,
        vector,
        matrix,
        vector,
        vector,
        vector,
    )
    return jax.shard_map(
        functools.partial(per_device, grid),
        mesh=mesh,
        in_specs=(matrix, P("page", None), P("page", "band")) + parameters + (matrix,),
        out_specs=(matrix, matrix) + parameters,
        check_vma=False,
    )
```

time: 383 us -> 344 us (0.90)
  Pallas kernels: 33.9 us -> 102 us
  matrix products: 55.6 us -> 0 us
  local copies, waits for them, and re-layouts: 60.2 us -> 11.5 us
  starting transfers between devices: 68.7 us -> 97.7 us
  waiting for transfers between devices: 125 us -> 108 us
  other arithmetic: 30.9 us -> 19 us
    pallas_call x2 -> x8, Pallas kernels: 33.9 us -> 102 us  [the longest x2 21.5 us: attend_back(): pl.pallas_call(functools.partial(attend_back_kernel, start), grid=(pairs,...]
    dot_general x15 -> x0, matrix products: 55.6 us -> none  [the longest x6 23.3 us: outer_sum(): lax.dot_general(left, right, (((0,), (0,)), ((), ())), preferred_element_...]
    ppermute x45, starting transfers between devices: 68.7 us -> 97.7 us  [permute(): return lax.ppermute(array, AXES, pairs)]
    dynamic_update_slice x33 -> x12, local copies, waits for them, and re-layouts: 26.4 us -> 1.09 us  [__init__(): lax.dynamic_update_slice(block, piece[None], ((z - step) % grid.bands, 0,...]
    ppermute x45, waiting for transfers between devices: 125 us -> 108 us  [permute(): return lax.ppermute(array, AXES, pairs)]
    another operation x25 -> x3, other arithmetic: 13.3 us -> 0.34 us  [near_step(): self.near_all = jnp.stack([self.block] + got)]
    broadcast_in_dim x6 -> x3, local copies, waits for them, and re-layouts: 7.7 us -> 0.13 us  [__init__(): block = jnp.zeros((grid.bands, rows, width), pieces[0].dtype)]
    slice x10 -> x3, local copies, waits for them, and re-layouts: 7.58 us -> 1.03 us  [the longest x1 0.64 us: per_device(): d_a[:, :width]]
  transfers between devices with their start and end apart: 45 -> 45, of which waited for: 16 -> 24; matrix products, arithmetic and copies ran while one was open for 20% -> 5% of each run, Pallas kernels for 4% -> 14%
where the time goes in v2:
time: 344 us; the launch traced here: 340 us
  waiting for transfers between devices  108 us (31%)
  Pallas kernels  102 us (30%)
  starting transfers between devices  97.7 us (28%)
  other arithmetic  19 us (6%)
  local copies, waits for them, and re-layouts  11.5 us (3%)
    ppermute x45, waiting for transfers between devices, permute(): return lax.ppermute(array, AXES, pairs)  108 us
    ppermute x45, starting transfers between devices, permute(): return lax.ppermute(array, AXES, pairs)  97.7 us
    pallas_call x2, Pallas kernels, attend_back(): pl.pallas_call(functools.partial(attend_back_kernel, start), grid=(pairs,...  21.5 us
    pallas_call x1, Pallas kernels, dense_back(): pl.pallas_call(functools.partial(dense_back_kernel, grid, len(parts_b)),...  20.7 us
    pallas_call x1, Pallas kernels, middle(): pl.pallas_call(functools.partial(middle_kernel, grid, len(parts_b)), in_s...  20.3 us
    pallas_call x1, Pallas kernels, attend(): pl.pallas_call(functools.partial(attend_kernel, grid, pieces, len(parts))...  17.1 us
    pallas_call x1, Pallas kernels, weight_back(): pl.pallas_call(functools.partial(weight_back_kernel, grid, pieces), in_sp...  11.1 us
    pallas_call x1, Pallas kernels, input_back(): pl.pallas_call(functools.partial(input_back_kernel, grid, len(parts)), in...  9.49 us
  transfers between devices with their start and end apart: 45, of which 24 were waited for; matrix products, arithmetic and copies ran while one was open for 5% of the time, Pallas kernels for 14%

profile of v2, /device:TPU:0, one launch (start us, length us, event | category | flops | bytes accessed | tf_op | source)
XLA Modules:
  0.0 340.3 jit_solution(11306488387079493441)
XLA Ops:
  2.8 3.1 collective-permute-start
  12.4 5.3 %collective-permute-done.1 = bf16[24,2560]{1,0:T(8,128)(2,1)S(1)} collective-permute-done((bf16[24,2560]{1,0:T(8,128)(2,1)}, bf16[24,2560]{1,0:T(8,128)(2,1)S(1)}, u32[]{:S(2)}, u32[]{:S(2)}) %collective-permute-start.1) | collective-permute-done | bytes 122912 | tf_op jit(solution)/shard_map/ppermute | solution.py:51
  17.6 16.7 %collective-permute-start.3 = (bf16[24,3840]{1,0:T(8,128)(2,1)}, bf16[24,3840]{1,0:T(8,128)(2,1)S(1)}, u32[]{:S(2)}, u32[]{:S(2)}) collective-permute-start(bf16[24,3840]{1,0:T(8,128)(2,1)} %get-tuple-element.92), channel_id=1, source_target_pairs={{0,1},{1,2},{2,3},{3,0},{4,5},{5,6},{6,7},{7,4},{8,9},{9,10},{10,1... | collective-permute-start | bytes 552968 | tf_op jit(solution)/shard_map/ppermute | solution.py:51
  39.7 5.8 %collective-permute-done.4 = bf16[24,3840]{1,0:T(8,128)(2,1)S(1)} collective-permute-done((bf16[24,3840]{1,0:T(8,128)(2,1)}, bf16[24,3840]{1,0:T(8,128)(2,1)S(1)}, u32[]{:S(2)}, u32[]{:S(2)}) %collective-permute-start.4) | collective-permute-done | bytes 184352 | tf_op jit(solution)/shard_map/ppermute | solution.py:51
  48.4 4.3 %collective-permute-start.7 = (bf16[96,768]{1,0:T(8,128)(2,1)S(1)}, bf16[96,768]{1,0:T(8,128)(2,1)S(1)}, u32[]{:S(2)}, u32[]{:S(2)}) collective-permute-start(bf16[96,768]{1,0:T(8,128)(2,1)S(1)} %copy-done.19), channel_id=1, source_target_pairs={{0,1},{1,2},{2,3},{3,0},{4,5},{5,6},{6,7},{7,4},{8,9},{9,10},{10,1... | collective-permute-start | bytes 442376 | tf_op jit(solution)/shard_map/ppermute | solution.py:51
  52.7 3.3 collective-permute-start.8
  57.6 2.7 collective-permute-done.7
  61.8 3.3 collective-permute-done.8
  65.3 4.8 %collective-permute-done.10.refs_5_.refs_1_ = bf16[2,96,2560]{2,1,0:T(8,128)(2,1)S(1)} collective-permute-done((bf16[2,96,2560]{2,1,0:T(8,128)(2,1)S(1)}, bf16[2,96,2560]{2,1,0:T(8,128)(2,1)S(1)}, u32[]{:S(2)}, u32[]{:S(2)}) %collective-permute-start.10) | collective-permute-done | bytes 983072 | tf_op jit(solution)/shard_map/ppermute | solution.py:51
  74.6 13.3 %collective-permute-done.11 = bf16[384,768]{1,0:T(8,128)(2,1)S(1)} collective-permute-done((bf16[384,768]{1,0:T(8,128)(2,1)S(1)}, bf16[384,768]{1,0:T(8,128)(2,1)S(1)}, u32[]{:S(2)}, u32[]{:S(2)}) %collective-permute-start.11) | collective-permute-done | bytes 589856 | tf_op jit(solution)/shard_map/ppermute | solution.py:51
  91.3 14.6 %collective-permute-done.15.refs_3_ = bf16[320,768]{1,0:T(8,128)(2,1)S(1)} collective-permute-done((bf16[320,768]{1,0:T(8,128)(2,1)}, bf16[320,768]{1,0:T(8,128)(2,1)S(1)}, u32[]{:S(2)}, u32[]{:S(2)}) %collective-permute-start.15) | collective-permute-done | bytes 491552 | tf_op jit(solution)/shard_map/ppermute | solution.py:51
  107.9 17.1 %attend.1 = (bf16[320,768]{1,0:T(8,128)(2,1)}, bf16[1280,1536]{1,0:T(8,128)(2,1)}, bf16[320,768]{1,0:T(8,128)(2,1)}, f32[3,320,128]{2,1,0:T(8,128)}, f32[16,768]{1,0:T(8,128)}, /*index=5*/f32[1,3072]{1,0:T(1,128)}) custom-call(bf16[320,768]{1,0:T(8,128)(2,1)} %refs_0_.3, bf16[320,768]{1,0:T(8,128)(2,1)} %copy-done.10, ...), custom_call_target="tpu_custom_call" | custom-call | flops 1024 | bytes 1024 | tf_op jit(solution)/shard_map/attend/pallas_call | solution.py:342
  125.1 3.0 collective-permute-done.23.refs_7_
  129.1 20.3 %middle.1 = (bf16[320,768]{1,0:T(8,128)(2,1)}, bf16[320,768]{1,0:T(8,128)(2,1)}, f32[320,768]{1,0:T(8,128)}, f32[320,128]{1,0:T(8,128)}, bf16[320,3072]{1,0:T(8,...) custom-call(bf16[320,768]{1,0:T(8,128)(2,1)} %get-tuple-element.99.a, ...), custom_call_target="tpu_custom_call" | custom-call | flops 1024 | bytes 1024 | tf_op jit(solution)/shard_map/middle/pallas_call | solution.py:522
  149.7 4.5 %collective-permute-done.24 = bf16[4,384,768]{2,1,0:T(8,128)(2,1)S(1)} collective-permute-done((bf16[4,384,768]{2,1,0:T(8,128)(2,1)}, bf16[4,384,768]{2,1,0:T(8,128)(2,1)S(1)}, u32[]{:S(2)}, u32[]{:S(2)}) %collective-permute-start.24) | collective-permute-done | bytes 2359328 | tf_op jit(solution)/shard_map/ppermute | solution.py:51
  156.6 20.7 %dense_back.1 = (f32[320,768]{1,0:T(8,128)}, bf16[320,768]{1,0:T(8,128)(2,1)}, bf16[4,96,3840]{2,1,0:T(8,128)(2,1)}, bf16[4,96,3840]{2,1,0:T(8,128)(2,1)}, f32[8,768]{1,0:T(8,128)}, /*index=5*/f32[1,3072]{1,0:T(1,128)}) custom-call(bf16[320,768]{1,0:T(8,128)(2,1)} %get-tuple-element.99.att, bf16[320,768]{1,0:T(8,128)(2,1)} %get-tuple-element.105.first, ...), custom_call_target="tpu_custom_call" | custom-call | flops 1024 | bytes 1024 | tf_op jit(solution)/shard_map/dense_back/pallas_call | solution.py:590
  179.3 14.7 %collective-permute-done.25 = bf16[2,384,768]{2,1,0:T(8,128)(2,1)S(1)} collective-permute-done((bf16[2,384,768]{2,1,0:T(8,128)(2,1)S(1)}, bf16[2,384,768]{2,1,0:T(8,128)(2,1)S(1)}, u32[]{:S(2)}, u32[]{:S(2)}) %collective-permute-start.25) | collective-permute-done | bytes 1179680 | tf_op jit(solution)/shard_map/ppermute | solution.py:51
  196.5 10.8 %attend_back.2 = (bf16[320,384]{1,0:T(8,128)(2,1)}, bf16[1280,768]{1,0:T(8,128)(2,1)}, f32[8,384]{1,0:T(8,128)}) custom-call(bf16[320,768]{1,0:T(8,128)(2,1)} %get-tuple-element.115.q, bf16[1280,1536]{1,0:T(8,128)(2,1)} %get-tuple-element.116.kv, bf16[320,768]{1,0:T(8,128)(2,1)} %get-tuple-element.131.grad, bf16[320,768]{1,0:T(8,128)(2,1)} %get-tuple-element.99.att, ...), custom_call_target="tpu_custom_call" | custom-call | flops 1024 | bytes 1024 | tf_op jit(solution)/shard_map/attend_back/pallas_call | solution.py:414
  213.1 10.7 %attend_back.3 = (bf16[320,384]{1,0:T(8,128)(2,1)}, bf16[1280,768]{1,0:T(8,128)(2,1)}, f32[8,384]{1,0:T(8,128)}) custom-call(bf16[320,768]{1,0:T(8,128)(2,1)} %get-tuple-element.115.q, bf16[1280,1536]{1,0:T(8,128)(2,1)} %get-tuple-element.116.kv, bf16[320,768]{1,0:T(8,128)(2,1)} %get-tuple-element.131.grad, bf16[320,768]{1,0:T(8,128)(2,1)} %get-tuple-element.99.att, ...), custom_call_target="tpu_custom_call" | custom-call | flops 1024 | bytes 1024 | tf_op jit(solution)/shard_map/attend_back/pallas_call | solution.py:414
  223.8 9.5 %input_back.1 = (f32[320,768]{1,0:T(8,128)}, bf16[320,768]{1,0:T(8,128)(2,1)}, bf16[320,768]{1,0:T(8,128)(2,1)}, bf16[320,768]{1,0:T(8,128)(2,1)}) custom-call(f32[320,768]{1,0:T(8,128)} %get-tuple-element.114.grad_sum, bf16[320,384]{1,0:T(8,128)(2,1)} %get-tuple-element.122.dq0.refs_4_, bf16[320,384]{1,0:T(8,128)(2,1)} %get-tuple-element.141.dq1.refs_5_, ...), custom_call_target="tpu_custom_call" | custom-call | flops 1024 | bytes 1024 | tf_op jit(solution)/shard_map/input_back/pallas_call | solution.py:640
  233.3 2.8 fusion
  236.1 11.1 %weight_back.1 = (bf16[4,96,2560]{2,1,0:T(8,128)(2,1)}, bf16[4,96,2560]{2,1,0:T(8,128)(2,1)}) custom-call(bf16[320,768]{1,0:T(8,128)(2,1)} %refs_0_.3, bf16[320,768]{1,0:T(8,128)(2,1)} %copy-done.10, bf16[320,768]{1,0:T(8,128)(2,1)} %collective-permute-done.14.refs_2_, bf16[320,768]{1,0:T(8,128)(2,1)} %copy-done.11, ...), custom_call_target="tpu_custom_call" | custom-call | flops 1024 | bytes 1024 | tf_op jit(solution)/shard_map/weight_back/pallas_call | solution.py:687
  249.7 3.2 collective-permute-start.44
  252.9 11.6 %collective-permute-done.42 = bf16[96,768]{1,0:T(8,128)(2,1)S(1)} collective-permute-done((bf16[96,768]{1,0:T(8,128)(2,1)}, bf16[96,768]{1,0:T(8,128)(2,1)S(1)}, u32[]{:S(2)}, u32[]{:S(2)}) %collective-permute-start.42) | collective-permute-done | bytes 147488 | tf_op jit(solution)/shard_map/ppermute | solution.py:51
  264.5 5.1 %collective-permute-done.43 = bf16[96,768]{1,0:T(8,128)(2,1)S(1)} collective-permute-done((bf16[96,768]{1,0:T(8,128)(2,1)}, bf16[96,768]{1,0:T(8,128)(2,1)S(1)}, u32[]{:S(2)}, u32[]{:S(2)}) %collective-permute-start.43) | collective-permute-done | bytes 147488 | tf_op jit(solution)/shard_map/ppermute | solution.py:51
  274.2 5.5 %collective-permute-start.32 = (bf16[320,768]{1,0:T(8,128)(2,1)S(1)}, bf16[320,768]{1,0:T(8,128)(2,1)S(1)}, u32[]{:S(2)}, u32[]{:S(2)}) collective-permute-start(bf16[320,768]{1,0:T(8,128)(2,1)S(1)} %add_convert_fusion.8), channel_id=1, source_target_pairs={{0,3},{1,0},{2,1},{3,2},{4,7},{5,4},{6,5},{7,6},{8,11},{9,8},{10,9... | collective-permute-start | bytes 1474568 | tf_op jit(solution)/shard_map/ppermute | solution.py:51
  281.7 3.5 %collective-permute-done.31 = bf16[96,3840]{1,0:T(8,128)(2,1)S(1)} collective-permute-done((bf16[96,3840]{1,0:T(8,128)(2,1)}, bf16[96,3840]{1,0:T(8,128)(2,1)S(1)}, u32[]{:S(2)}, u32[]{:S(2)}) %collective-permute-start.31) | collective-permute-done | bytes 737312 | tf_op jit(solution)/shard_map/ppermute | solution.py:51
  287.0 7.8 %collective-permute-start.39 = (bf16[24,3840]{1,0:T(8,128)(2,1)S(1)}, bf16[24,3840]{1,0:T(8,128)(2,1)S(1)}, u32[]{:S(2)}, u32[]{:S(2)}) collective-permute-start(bf16[24,3840]{1,0:T(8,128)(2,1)S(1)} %get-tuple-element.173), channel_id=1, source_target_pairs={{0,1},{1,2},{2,3},{3,0},{4,5},{5,6},{6,7},{7,4},{8,9},{9,10},{10,1... | collective-permute-start | bytes 552968 | tf_op jit(solution)/shard_map/ppermute | solution.py:51
  294.8 3.3 collective-permute-start.40
  303.1 4.3 %collective-permute-done.40 = bf16[24,3840]{1,0:T(8,128)(2,1)S(1)} collective-permute-done((bf16[24,3840]{1,0:T(8,128)(2,1)S(1)}, bf16[24,3840]{1,0:T(8,128)(2,1)S(1)}, u32[]{:S(2)}, u32[]{:S(2)}) %collective-permute-start.40) | collective-permute-done | bytes 184352 | tf_op jit(solution)/shard_map/ppermute | solution.py:51
  311.3 15.5 %collective-permute-start.36 = (bf16[24,2560]{1,0:T(8,128)(2,1)S(1)}, bf16[24,2560]{1,0:T(8,128)(2,1)S(1)}, u32[]{:S(2)}, u32[]{:S(2)}) collective-permute-start(bf16[24,2560]{1,0:T(8,128)(2,1)S(1)} %get-tuple-element.177), channel_id=1, source_target_pairs={{0,1},{1,2},{2,3},{3,0},{4,5},{5,6},{6,7},{7,4},{8,9},{9,10},{10,1... | collective-permute-start | bytes 368648 | tf_op jit(solution)/shard_map/ppermute | solution.py:51
  326.7 3.4 collective-permute-start.37
  (164 shorter events, 73.8 us)
Async XLA Ops:
  9.8 62.4 %collective-permute-start.13 = (bf16[320,768]{1,0:T(8,128)(2,1)}, bf16[320,768]{1,0:T(8,128)(2,1)S(1)}, u32[]{:S(2)}, u32[]{:S(2)}) collective-permute-start(bf16[320,768]{1,0:T(8,128)(2,1)} %refs_0_.3), channel_id=1, source_target_pairs={{0,1},{1,2},{2,3},{3,0},{4,5},{5,6},{6,7},{7,4},{8,9},{9,10},{10,1... | collective-permute-start | bytes 1474568 | tf_op jit(solution)/shard_map/ppermute | solution.py:51
  17.6 22.1 %collective-permute-start.3 = (bf16[24,3840]{1,0:T(8,128)(2,1)}, bf16[24,3840]{1,0:T(8,128)(2,1)S(1)}, u32[]{:S(2)}, u32[]{:S(2)}) collective-permute-start(bf16[24,3840]{1,0:T(8,128)(2,1)} %get-tuple-element.92), channel_id=1, source_target_pairs={{0,1},{1,2},{2,3},{3,0},{4,5},{5,6},{6,7},{7,4},{8,9},{9,10},{10,1... | collective-permute-start | bytes 552968 | tf_op jit(solution)/shard_map/ppermute | solution.py:51
  34.4 12.3 %collective-permute-start.5 = (bf16[24,3840]{1,0:T(8,128)(2,1)}, bf16[24,3840]{1,0:T(8,128)(2,1)S(1)}, u32[]{:S(2)}, u32[]{:S(2)}) collective-permute-start(bf16[24,3840]{1,0:T(8,128)(2,1)} %get-tuple-element.92), channel_id=1, source_target_pairs={{0,3},{1,0},{2,1},{3,2},{4,7},{5,4},{6,5},{7,6},{8,11},{9,8},{10,9... | collective-permute-start | bytes 552968 | tf_op jit(solution)/shard_map/ppermute | solution.py:51
  46.7 18.4 %collective-permute-start.12 = (bf16[96,3840]{1,0:T(8,128)(2,1)S(1)}, bf16[96,3840]{1,0:T(8,128)(2,1)S(1)}, u32[]{:S(2)}, u32[]{:S(2)}) collective-permute-start(bf16[96,3840]{1,0:T(8,128)(2,1)S(1)} %bitcast.117), channel_id=1, source_target_pairs={{0,8},{1,9},{2,10},{3,11},{4,20},{5,21},{6,22},{7,23},{8,0},{9,1},... | collective-permute-start | bytes 2211848 | tf_op jit(solution)/shard_map/ppermute | solution.py:51
  52.7 12.4 %collective-permute-start.8 = (bf16[96,768]{1,0:T(8,128)(2,1)S(1)}, bf16[96,768]{1,0:T(8,128)(2,1)S(1)}, u32[]{:S(2)}, u32[]{:S(2)}) collective-permute-start(bf16[96,768]{1,0:T(8,128)(2,1)S(1)} %copy-done.19), channel_id=1, source_target_pairs={{0,2},{1,3},{2,0},{3,1},{4,6},{5,7},{6,4},{7,5},{8,10},{9,11},{10,... | collective-permute-start | bytes 442376 | tf_op jit(solution)/shard_map/ppermute | solution.py:51
  56.0 14.1 %collective-permute-start.10 = (bf16[2,96,2560]{2,1,0:T(8,128)(2,1)S(1)}, bf16[2,96,2560]{2,1,0:T(8,128)(2,1)S(1)}, u32[]{:S(2)}, u32[]{:S(2)}) collective-permute-start(bf16[2,96,2560]{2,1,0:T(8,128)(2,1)S(1)} %pad_maximum_fusion.2.refs_4_.refs_0_), channel_id=1, source_target_pairs={{0,16},{1,17},{2,18},{3,19},{4,12},{5,13},{6,14},{7,15},{8,24},{9,... | collective-permute-start | bytes 2949128 | tf_op jit(solution)/shard_map/ppermute | solution.py:51
  70.1 35.8 %collective-permute-start.18 = (bf16[2,96,3840]{2,1,0:T(8,128)(2,1)S(1)}, bf16[2,96,3840]{2,1,0:T(8,128)(2,1)}, u32[]{:S(2)}, u32[]{:S(2)}) collective-permute-start(bf16[2,96,3840]{2,1,0:T(8,128)(2,1)S(1)} %pad_maximum_fusion.refs_0_), channel_id=1, source_target_pairs={{0,16},{1,17},{2,18},{3,19},{4,12},{5,13},{6,14},{7,15},{8,24},{9,... | collective-permute-start | bytes 4423688 | tf_op jit(solution)/shard_map/ppermute | solution.py:51
  71.6 16.3 %collective-permute-start.11 = (bf16[384,768]{1,0:T(8,128)(2,1)S(1)}, bf16[384,768]{1,0:T(8,128)(2,1)S(1)}, u32[]{:S(2)}, u32[]{:S(2)}) collective-permute-start(bf16[384,768]{1,0:T(8,128)(2,1)S(1)} %bitcast.121), channel_id=1, source_target_pairs={{0,8},{1,9},{2,10},{3,11},{4,20},{5,21},{6,22},{7,23},{8,0},{9,1},... | collective-permute-start | bytes 1769480 | tf_op jit(solution)/shard_map/ppermute | solution.py:51
  72.2 17.2 %collective-permute-start.14 = (bf16[320,768]{1,0:T(8,128)(2,1)S(1)}, bf16[320,768]{1,0:T(8,128)(2,1)}, u32[]{:S(2)}, u32[]{:S(2)}) collective-permute-start(bf16[320,768]{1,0:T(8,128)(2,1)S(1)} %collective-permute-done.13.refs_1_), channel_id=1, source_target_pairs={{0,1},{1,2},{2,3},{3,0},{4,5},{5,6},{6,7},{7,4},{8,9},{9,10},{10,1... | collective-permute-start | bytes 1474568 | tf_op jit(solution)/shard_map/ppermute | solution.py:51
  88.1 36.9 %collective-permute-start.21 = (bf16[2,384,768]{2,1,0:T(8,128)(2,1)S(1)}, bf16[2,384,768]{2,1,0:T(8,128)(2,1)}, u32[]{:S(2)}, u32[]{:S(2)}) collective-permute-start(bf16[2,384,768]{2,1,0:T(8,128)(2,1)S(1)} %pad_maximum_fusion.1.refs_4_), channel_id=1, source_target_pairs={{0,16},{1,17},{2,18},{3,19},{4,12},{5,13},{6,14},{7,15},{8,24},{9,... | collective-permute-start | bytes 3538952 | tf_op jit(solution)/shard_map/ppermute | solution.py:51
  89.4 17.9 %collective-permute-start.16 = (bf16[2,96,2560]{2,1,0:T(8,128)(2,1)}, bf16[2,96,2560]{2,1,0:T(8,128)(2,1)}, u32[]{:S(2)}, u32[]{:S(2)}) collective-permute-start(bf16[2,96,2560]{2,1,0:T(8,128)(2,1)} %copy-done.2), channel_id=1, source_target_pairs={{0,4},{1,5},{2,6},{3,7},{4,0},{5,1},{6,2},{7,3},{8,12},{9,13},{10,... | collective-permute-start | bytes 2949128 | tf_op jit(solution)/shard_map/ppermute | solution.py:51
  89.5 16.4 %collective-permute-start.15 = (bf16[320,768]{1,0:T(8,128)(2,1)}, bf16[320,768]{1,0:T(8,128)(2,1)S(1)}, u32[]{:S(2)}, u32[]{:S(2)}) collective-permute-start(bf16[320,768]{1,0:T(8,128)(2,1)} %collective-permute-done.14.refs_2_), channel_id=1, source_target_pairs={{0,1},{1,2},{2,3},{3,0},{4,5},{5,6},{6,7},{7,4},{8,9},{9,10},{10,1... | collective-permute-start | bytes 1474568 | tf_op jit(solution)/shard_map/ppermute | solution.py:51
  91.0 16.8 %collective-permute-start.17 = (bf16[2,96,2560]{2,1,0:T(8,128)(2,1)}, bf16[2,96,2560]{2,1,0:T(8,128)(2,1)}, u32[]{:S(2)}, u32[]{:S(2)}) collective-permute-start(bf16[2,96,2560]{2,1,0:T(8,128)(2,1)} %copy-done.5), channel_id=1, source_target_pairs={{0,4},{1,5},{2,6},{3,7},{4,0},{5,1},{6,2},{7,3},{8,12},{9,13},{10,... | collective-permute-start | bytes 2949128 | tf_op jit(solution)/shard_map/ppermute | solution.py:51
  105.9 19.2 %collective-permute-start.19 = (bf16[2,96,3840]{2,1,0:T(8,128)(2,1)S(1)}, bf16[2,96,3840]{2,1,0:T(8,128)(2,1)}, u32[]{:S(2)}, u32[]{:S(2)}) collective-permute-start(bf16[2,96,3840]{2,1,0:T(8,128)(2,1)S(1)} %pad_maximum_fusion.refs_0_), channel_id=1, source_target_pairs={{0,4},{1,5},{2,6},{3,7},{4,0},{5,1},{6,2},{7,3},{8,12},{9,13},{10,... | collective-permute-start | bytes 4423688 | tf_op jit(solution)/shard_map/ppermute | solution.py:51
  106.6 21.5 %collective-permute-start.20 = (bf16[2,96,3840]{2,1,0:T(8,128)(2,1)}, bf16[2,96,3840]{2,1,0:T(8,128)(2,1)}, u32[]{:S(2)}, u32[]{:S(2)}) collective-permute-start(bf16[2,96,3840]{2,1,0:T(8,128)(2,1)} %collective-permute-done.18.refs_1_), channel_id=1, source_target_pairs={{0,4},{1,5},{2,6},{3,7},{4,0},{5,1},{6,2},{7,3},{8,12},{9,13},{10,... | collective-permute-start | bytes 4423688 | tf_op jit(solution)/shard_map/ppermute | solution.py:51
  107.4 17.7 %collective-permute-start.22 = (bf16[2,384,768]{2,1,0:T(8,128)(2,1)S(1)}, bf16[2,384,768]{2,1,0:T(8,128)(2,1)S(1)}, u32[]{:S(2)}, u32[]{:S(2)}) collective-permute-start(bf16[2,384,768]{2,1,0:T(8,128)(2,1)S(1)} %pad_maximum_fusion.1.refs_4_), channel_id=1, source_target_pairs={{0,4},{1,5},{2,6},{3,7},{4,0},{5,1},{6,2},{7,3},{8,12},{9,13},{10,... | collective-permute-start | bytes 3538952 | tf_op jit(solution)/shard_map/ppermute | solution.py:51
  177.3 32.5 %collective-permute-start.27 = (bf16[4,96,3840]{2,1,0:T(8,128)(2,1)}, bf16[4,96,3840]{2,1,0:T(8,128)(2,1)}, u32[]{:S(2)}, u32[]{:S(2)}) collective-permute-start(bf16[4,96,3840]{2,1,0:T(8,128)(2,1)} %get-tuple-element.130), channel_id=1, source_target_pairs={{0,4},{1,5},{2,6},{3,7},{4,0},{5,1},{6,2},{7,3},{8,12},{9,13},{10,... | collective-permute-start | bytes 8847368 | tf_op jit(solution)/shard_map/ppermute | solution.py:51
  177.7 16.2 %collective-permute-start.25 = (bf16[2,384,768]{2,1,0:T(8,128)(2,1)S(1)}, bf16[2,384,768]{2,1,0:T(8,128)(2,1)S(1)}, u32[]{:S(2)}, u32[]{:S(2)}) collective-permute-start(bf16[2,384,768]{2,1,0:T(8,128)(2,1)S(1)} %add_convert_fusion.1), channel_id=1, source_target_pairs={{0,16},{1,17},{2,18},{3,19},{4,12},{5,13},{6,14},{7,15},{8,24},{9,... | collective-permute-start | bytes 3538952 | tf_op jit(solution)/shard_map/ppermute | solution.py:51
  195.0 12.3 %collective-permute-start.26 = (bf16[384,768]{1,0:T(8,128)(2,1)S(1)}, bf16[384,768]{1,0:T(8,128)(2,1)}, u32[]{:S(2)}, u32[]{:S(2)}) collective-permute-start(bf16[384,768]{1,0:T(8,128)(2,1)S(1)} %fusion.1), channel_id=1, source_target_pairs={{0,8},{1,9},{2,10},{3,11},{4,20},{5,21},{6,22},{7,23},{8,0},{9,1},... | collective-permute-start | bytes 1769480 | tf_op jit(solution)/shard_map/ppermute | solution.py:51
  211.5 21.8 %collective-permute-start.28 = (bf16[2,96,3840]{2,1,0:T(8,128)(2,1)S(1)}, bf16[2,96,3840]{2,1,0:T(8,128)(2,1)S(1)}, u32[]{:S(2)}, u32[]{:S(2)}) collective-permute-start(bf16[2,96,3840]{2,1,0:T(8,128)(2,1)S(1)} %add_convert_fusion), channel_id=1, source_target_pairs={{0,16},{1,17},{2,18},{3,19},{4,12},{5,13},{6,14},{7,15},{8,24},{9,... | collective-permute-start | bytes 4423688 | tf_op jit(solution)/shard_map/ppermute | solution.py:51
  247.3 32.4 %collective-permute-start.30 = (bf16[4,96,2560]{2,1,0:T(8,128)(2,1)}, bf16[4,96,2560]{2,1,0:T(8,128)(2,1)}, u32[]{:S(2)}, u32[]{:S(2)}) collective-permute-start(bf16[4,96,2560]{2,1,0:T(8,128)(2,1)} %get-tuple-element.150), channel_id=1, source_target_pairs={{0,4},{1,5},{2,6},{3,7},{4,0},{5,1},{6,2},{7,3},{8,12},{9,13},{10,... | collective-permute-start | bytes 5898248 | tf_op jit(solution)/shard_map/ppermute | solution.py:51
  247.3 25.6 %collective-permute-start.29 = (bf16[320,768]{1,0:T(8,128)(2,1)}, bf16[320,768]{1,0:T(8,128)(2,1)}, u32[]{:S(2)}, u32[]{:S(2)}) collective-permute-start(bf16[320,768]{1,0:T(8,128)(2,1)} %get-tuple-element.137), channel_id=1, source_target_pairs={{0,3},{1,0},{2,1},{3,2},{4,7},{5,4},{6,5},{7,6},{8,11},{9,8},{10,9... | collective-permute-start | bytes 1474568 | tf_op jit(solution)/shard_map/ppermute | solution.py:51
  249.1 15.4 %collective-permute-start.42 = (bf16[96,768]{1,0:T(8,128)(2,1)}, bf16[96,768]{1,0:T(8,128)(2,1)S(1)}, u32[]{:S(2)}, u32[]{:S(2)}) collective-permute-start(bf16[96,768]{1,0:T(8,128)(2,1)} %get-tuple-element.176), channel_id=1, source_target_pairs={{0,1},{1,2},{2,3},{3,0},{4,5},{5,6},{6,7},{7,4},{8,9},{9,10},{10,1... | collective-permute-start | bytes 442376 | tf_op jit(solution)/shard_map/ppermute | solution.py:51
  249.4 20.2 %collective-permute-start.43 = (bf16[96,768]{1,0:T(8,128)(2,1)}, bf16[96,768]{1,0:T(8,128)(2,1)S(1)}, u32[]{:S(2)}, u32[]{:S(2)}) collective-permute-start(bf16[96,768]{1,0:T(8,128)(2,1)} %get-tuple-element.175), channel_id=1, source_target_pairs={{0,2},{1,3},{2,0},{3,1},{4,6},{5,7},{6,4},{7,5},{8,10},{9,11},{10,... | collective-permute-start | bytes 442376 | tf_op jit(solution)/shard_map/ppermute | solution.py:51
  249.7 21.0 %collective-permute-start.44 = (bf16[96,768]{1,0:T(8,128)(2,1)}, bf16[96,768]{1,0:T(8,128)(2,1)}, u32[]{:S(2)}, u32[]{:S(2)}) collective-permute-start(bf16[96,768]{1,0:T(8,128)(2,1)} %get-tuple-element.174), channel_id=1, source_target_pairs={{0,3},{1,0},{2,1},{3,2},{4,7},{5,4},{6,5},{7,6},{8,11},{9,8},{10,9... | collective-permute-start | bytes 442376 | tf_op jit(solution)/shard_map/ppermute | solution.py:51
  272.4 12.8 %collective-permute-start.31 = (bf16[96,3840]{1,0:T(8,128)(2,1)}, bf16[96,3840]{1,0:T(8,128)(2,1)S(1)}, u32[]{:S(2)}, u32[]{:S(2)}) collective-permute-start(bf16[96,3840]{1,0:T(8,128)(2,1)} %fusion), channel_id=1, source_target_pairs={{0,8},{1,9},{2,10},{3,11},{4,20},{5,21},{6,22},{7,23},{8,0},{9,1},... | collective-permute-start | bytes 2211848 | tf_op jit(solution)/shard_map/ppermute | solution.py:51
  274.2 23.9 %collective-permute-start.32 = (bf16[320,768]{1,0:T(8,128)(2,1)S(1)}, bf16[320,768]{1,0:T(8,128)(2,1)S(1)}, u32[]{:S(2)}, u32[]{:S(2)}) collective-permute-start(bf16[320,768]{1,0:T(8,128)(2,1)S(1)} %add_convert_fusion.8), channel_id=1, source_target_pairs={{0,3},{1,0},{2,1},{3,2},{4,7},{5,4},{6,5},{7,6},{8,11},{9,8},{10,9... | collective-permute-start | bytes 1474568 | tf_op jit(solution)/shard_map/ppermute | solution.py:51
  281.2 18.6 %collective-permute-start.34 = (bf16[2,96,2560]{2,1,0:T(8,128)(2,1)S(1)}, bf16[2,96,2560]{2,1,0:T(8,128)(2,1)S(1)}, u32[]{:S(2)}, u32[]{:S(2)}) collective-permute-start(bf16[2,96,2560]{2,1,0:T(8,128)(2,1)S(1)} %add_convert_fusion.2), channel_id=1, source_target_pairs={{0,16},{1,17},{2,18},{3,19},{4,12},{5,13},{6,14},{7,15},{8,24},{9,... | collective-permute-start | bytes 2949128 | tf_op jit(solution)/shard_map/ppermute | solution.py:51
  287.0 16.1 %collective-permute-start.39 = (bf16[24,3840]{1,0:T(8,128)(2,1)S(1)}, bf16[24,3840]{1,0:T(8,128)(2,1)S(1)}, u32[]{:S(2)}, u32[]{:S(2)}) collective-permute-start(bf16[24,3840]{1,0:T(8,128)(2,1)S(1)} %get-tuple-element.173), channel_id=1, source_target_pairs={{0,1},{1,2},{2,3},{3,0},{4,5},{5,6},{6,7},{7,4},{8,9},{9,10},{10,1... | collective-permute-start | bytes 552968 | tf_op jit(solution)/shard_map/ppermute | solution.py:51
  294.8 12.5 %collective-permute-start.40 = (bf16[24,3840]{1,0:T(8,128)(2,1)S(1)}, bf16[24,3840]{1,0:T(8,128)(2,1)S(1)}, u32[]{:S(2)}, u32[]{:S(2)}) collective-permute-start(bf16[24,3840]{1,0:T(8,128)(2,1)S(1)} %get-tuple-element.172), channel_id=1, source_target_pairs={{0,2},{1,3},{2,0},{3,1},{4,6},{5,7},{6,4},{7,5},{8,10},{9,11},{10,... | collective-permute-start | bytes 552968 | tf_op jit(solution)/shard_map/ppermute | solution.py:51
  298.2 31.9 %collective-permute-start.33 = (bf16[320,768]{1,0:T(8,128)(2,1)S(1)}, bf16[320,768]{1,0:T(8,128)(2,1)S(1)}, u32[]{:S(2)}, u32[]{:S(2)}) collective-permute-start(bf16[320,768]{1,0:T(8,128)(2,1)S(1)} %add_convert_fusion.7), channel_id=1, source_target_pairs={{0,3},{1,0},{2,1},{3,2},{4,7},{5,4},{6,5},{7,6},{8,11},{9,8},{10,9... | collective-permute-start | bytes 1474568 | tf_op jit(solution)/shard_map/ppermute | solution.py:51
  311.3 21.2 %collective-permute-start.36 = (bf16[24,2560]{1,0:T(8,128)(2,1)S(1)}, bf16[24,2560]{1,0:T(8,128)(2,1)S(1)}, u32[]{:S(2)}, u32[]{:S(2)}) collective-permute-start(bf16[24,2560]{1,0:T(8,128)(2,1)S(1)} %get-tuple-element.177), channel_id=1, source_target_pairs={{0,1},{1,2},{2,3},{3,0},{4,5},{5,6},{6,7},{7,4},{8,9},{9,10},{10,1... | collective-permute-start | bytes 368648 | tf_op jit(solution)/shard_map/ppermute | solution.py:51
  (34 other events, 533.3 us)
